TPU v7x, 128 devices: a whole 4x4x4 slice. The times are simulated.
128 devices in a mesh: grp: 2 (over x_hi), sp: 64 (over y, z, x_lo, core).
Axes of the slice: x: 4 (x_hi: 2, x_lo: 2; x = x_hi * 2 + x_lo), y: 4, z: 4, core: 2. Of those that a mesh axis runs over, the one named last changes fastest.
Arguments:
- positions: float32 [3, 262144], P(None, ('grp', 'sp')), may hold values from 0 to 2
- dipoles: float32 [3, 262144], P(None, ('grp', 'sp')), may hold values from -6 to 6
- spline_values: float32 [3, 4, 262144], P(None, None, ('grp', 'sp')), may hold values from 0 to 1
- spline_slopes: float32 [3, 4, 262144], P(None, None, ('grp', 'sp')), may hold values from -5 to 5
- plane_base: int32 [262144], P(('grp', 'sp')), may hold values from 0 to 383, as said below
- row_base: int32 [262144], P(('grp', 'sp')), may hold values from 0 to 255
- column_base: int32 [262144], P(('grp', 'sp')), may hold values from 0 to 255
- pair_home: int32 [4096], P(('grp', 'sp')), may hold values from 0 to 15
- pair_other: int32 [4096], P(('grp', 'sp')), may hold values from 0 to 47, as said below
- pair_count: int32 [128], P(('grp', 'sp')), may hold values from 6 to 32, as said below
- influence: float32 [384, 256, 256], P(None, ('grp', 'sp')), may hold values from 0.05 to 1
Outputs:
- field: float32 [3, 262144], P(None, ('grp', 'sp'))
Inputs may be any that keep to these rules, and one draw needn't show every extreme that they name: The atoms of cell d have plane_base from d * 3 to (d + 1) * 3 - 1. `pair_other`: slot t of a cell takes its source cluster from the lower neighbour cell, the own cell or the upper neighbour cell as t mod 3 is 0, 1 or 2. Slots d * 32 to d * 32 + pair_count[d] - 1 of cell d are live, the rest are ignored; some cell has all 32 slots live.
All inputs are finite; a program needn't handle non-finite values.
Results may differ from a plain program's by a relative error of at most 0.0003.
Values sent between devices are 32-bit elements; how exact they have to be, the bound alone decides.
A program may use at most 64 MiB of HBM per device.

v0:
```python
import math

import jax
import jax.numpy as jnp
from jax import lax
from jax.sharding import PartitionSpec as P

CL = 128
CLU_DEV = 16
GX = 384
GY = 256
GZ = 256


soften = 0.25
cell_width = 2.0
direct_scale = 0.125
slot_batch = 16
highest = lax.Precision.HIGHEST


def padded(x, sides, width):
    for axis, dim in sides:
        devices, length = (lax.axis_size(axis), x.shape[dim])
        up = [(i, (i + 1) % devices) for i in range(devices)]
        down = [(j, i) for i, j in up]
        last = lax.slice_in_dim(x, length - width, length, axis=dim)
        leading = lax.slice_in_dim(x, 0, width, axis=dim)
        before = lax.ppermute(last, axis, up)
        after = lax.ppermute(leading, axis, down)
        x = jnp.concatenate([before, x, after], axis=dim)
    return x


def passed_along(value, axis, steps):
    count = lax.axis_size(axis)
    pairs = [(source, (source + steps) % count) for source in range(count)]
    return lax.ppermute(value, axis, pairs)


def block_field(home_rows, other_rows, self_mask):
    delta = [
        home_rows[..., axis_index, :, None] - other_rows[..., axis_index, None, :]
        for axis_index in range(3)
    ]
    distance = delta[0] * delta[0] + delta[1] * delta[1] + delta[2] * delta[2]
    screen = jnp.exp(-0.5 * distance)
    inverse = lax.rsqrt(distance + soften)
    first = screen * inverse * inverse * inverse
    second = 3.0 * first * inverse * inverse
    width = home_rows.shape[-1]
    keeping = 1.0 - self_mask[..., None, None] * jnp.eye(width, dtype=jnp.float32)
    moment = [other_rows[..., 3 + axis_index, None, :] for axis_index in range(3)]
    along = delta[0] * moment[0] + delta[1] * moment[1] + delta[2] * moment[2]
    fields = [
        jnp.sum(
            keeping * (second * along * delta[axis_index] - first * moment[axis_index]), axis=-1
        )
        for axis_index in range(3)
    ]
    return jnp.stack(fields, axis=-2)


def stencil_weights(values, slopes, offset):
    weight_x = slopes[0, offset][None, None, :] * values[1][:, None, :] * values[2][None, :, :]
    weight_y = values[0, offset][None, None, :] * slopes[1][:, None, :] * values[2][None, :, :]
    weight_z = values[0, offset][None, None, :] * values[1][:, None, :] * slopes[2][None, :, :]
    return (weight_x, weight_y, weight_z)


def stencil_cells(plane, row_base, column_base):
    steps_four = jnp.arange(4, dtype=jnp.int32)[:, None]
    rows_all = (row_base[None, :] + steps_four) % GY
    columns_all = (column_base[None, :] + steps_four) % GZ
    return (plane[None, None, :] * GY + rows_all[:, None, :]) * GZ + columns_all[None, :, :]


def spread_into(grid, moments, values, slopes, local_plane, row_base, column_base, lift, limit):
    for offset in range(4):
        weight_x, weight_y, weight_z = stencil_weights(values, slopes, offset)
        plane = local_plane + offset + lift
        valid = ((plane >= 0) & (plane < limit)).astype(jnp.float32)
        cells = stencil_cells(jnp.clip(plane, 0, limit - 1), row_base, column_base)
        amount = (moments[0] * weight_x + moments[1] * weight_y + moments[2] * weight_z) * valid[
            None, None, :
        ]
        grid = grid.at[cells].add(amount)
    return grid


def sample_from(flat_potential, values, slopes, local_plane, row_base, column_base, lift, limit):
    recip = [jnp.zeros(local_plane.shape, jnp.float32) for component in range(3)]
    for offset in range(4):
        weights = stencil_weights(values, slopes, offset)
        plane = local_plane + offset + lift
        valid = ((plane >= 0) & (plane < limit)).astype(jnp.float32)
        cells = stencil_cells(jnp.clip(plane, 0, limit - 1), row_base, column_base)
        sampled = flat_potential[cells] * valid[None, None, :]
        for component in range(3):
            recip[component] = recip[component] - jnp.sum(weights[component] * sampled, axis=(0, 1))
    return jnp.stack(recip)


def dft_table(order, length):
    product = order[:, None] * jnp.arange(length, dtype=jnp.int32)[None, :] % length
    angle = product.astype(jnp.float32) * (2.0 * math.pi / length)
    return (jnp.cos(angle), jnp.sin(angle))


def along_z(field, table):
    return jnp.einsum("pyz,kz->pyk", field, table, precision=highest)


def along_y(field, table):
    return jnp.einsum("pyz,ky->pkz", field, table, precision=highest)


def forward_x(field, table):
    return jnp.einsum("qyz,qk->kyz", field, table, precision=highest)


def backward_x(field, table):
    return jnp.einsum("kyz,qk->qyz", field, table, precision=highest)


def on_device(
    positions,
    dipoles,
    spline_values,
    spline_slopes,
    plane_base,
    row_base,
    column_base,
    pair_home,
    pair_other,
    pair_count,
    influence,
):
    group_size = lax.axis_size("grp") * lax.axis_size("sp")
    planes = GX // group_size
    atom_total = positions.shape[1]
    stacked = jnp.concatenate([positions, dipoles], axis=0)
    extended = padded(stacked, ((("grp", "sp"), 1),), atom_total)
    shifts = jnp.concatenate(
        [
            jnp.full((atom_total,), -cell_width, jnp.float32),
            jnp.zeros((atom_total,), jnp.float32),
            jnp.full((atom_total,), cell_width, jnp.float32),
        ]
    )
    extended = extended.at[0].add(shifts)
    cluster_rows = extended.reshape(6, 3 * CLU_DEV, CL).transpose(1, 0, 2)
    slot_total = pair_count[0]
    turns = (slot_total + slot_batch - 1) // slot_batch

    def one_turn(step_index, totals):
        start = step_index * slot_batch
        homes = lax.dynamic_slice_in_dim(pair_home, start, slot_batch)
        others = lax.dynamic_slice_in_dim(pair_other, start, slot_batch)
        live_mask = (start + jnp.arange(slot_batch, dtype=jnp.int32) < slot_total).astype(
            jnp.float32
        )
        self_mask = (others == homes + CLU_DEV).astype(jnp.float32)
        blocks = (
            block_field(cluster_rows[homes + CLU_DEV], cluster_rows[others], self_mask)
            * live_mask[:, None, None]
        )
        return totals.at[homes].add(blocks)

    totals = lax.fori_loop(0, turns, one_turn, jnp.zeros((CLU_DEV, 3, CL), jnp.float32))
    direct = totals.transpose(1, 0, 2).reshape(3, atom_total)
    local_plane = plane_base % planes
    grid = jnp.zeros(((planes + 3) * GY * GZ,), jnp.float32)
    grid = spread_into(
        grid,
        dipoles,
        spline_values,
        spline_slopes,
        local_plane,
        row_base,
        column_base,
        0,
        planes + 3,
    )
    grid = grid.reshape(planes + 3, GY, GZ)
    incoming = passed_along(grid[planes:], ("grp", "sp"), 1)
    charge = grid[:planes].at[:3].add(incoming)
    cos_z, sin_z = dft_table(jnp.arange(GZ, dtype=jnp.int32), GZ)
    cos_y, sin_y = dft_table(jnp.arange(GY, dtype=jnp.int32), GY)
    real_part = along_z(charge, cos_z)
    imag_part = -along_z(charge, sin_z)
    real_next = along_y(real_part, cos_y) + along_y(imag_part, sin_y)
    imag_next = along_y(imag_part, cos_y) - along_y(real_part, sin_y)
    planes_grid = jnp.stack([real_next, imag_next])
    moved = lax.all_to_all(planes_grid, ("grp", "sp"), split_axis=2, concat_axis=1, tiled=True)
    order = jnp.arange(GX, dtype=jnp.int32)
    cos_x, sin_x = dft_table(order, GX)
    spec_real = (forward_x(moved[0], cos_x) + forward_x(moved[1], sin_x)) * influence
    spec_imag = (forward_x(moved[1], cos_x) - forward_x(moved[0], sin_x)) * influence
    back_real = backward_x(spec_real, cos_x) - backward_x(spec_imag, sin_x)
    back_imag = backward_x(spec_imag, cos_x) + backward_x(spec_real, sin_x)
    rows_grid = jnp.stack([back_real, back_imag])
    returned = lax.all_to_all(rows_grid, ("grp", "sp"), split_axis=1, concat_axis=2, tiled=True)
    real_back = along_y(returned[0], cos_y) - along_y(returned[1], sin_y)
    imag_back = along_y(returned[1], cos_y) + along_y(returned[0], sin_y)
    potential = (along_z(real_back, cos_z) - along_z(imag_back, sin_z)) * (1.0 / (GX * GY * GZ))
    upper_rim = passed_along(potential, ("grp", "sp"), -1)
    flat_potential = jnp.concatenate([potential, upper_rim], axis=0).reshape(-1)
    recip = sample_from(
        flat_potential,
        spline_values,
        spline_slopes,
        local_plane,
        row_base,
        column_base,
        0,
        planes + 3,
    )
    return direct_scale * direct + recip


def solution(mesh):
    placed = (
        P(None, ("grp", "sp")),
        P(None, ("grp", "sp")),
        P(None, None, ("grp", "sp")),
        P(None, None, ("grp", "sp")),
        P(("grp", "sp")),
        P(("grp", "sp")),
        P(("grp", "sp")),
        P(("grp", "sp")),
        P(("grp", "sp")),
        P(("grp", "sp")),
        P(None, ("grp", "sp"), None),
    )
    return jax.shard_map(
        on_device, mesh=mesh, in_specs=placed, out_specs=P(None, ("grp", "sp")), check_vma=False
    )
```

profile of v0, /device:TPU:0, one launch (start us, length us, event | category | flops | bytes accessed | tf_op | source)
XLA Modules:
  0.0 1592.3 jit_solution(12733886877305446011)
XLA Ops:
  0.0 1.4 pad_maximum_fusion.4
  1.4 8.2 collective-permute-start.1
  9.7 0.9 fusion.237
  10.6 0.9 fusion.236
  11.5 0.8 slice_bitcast_fusion
  12.3 0.9 fusion.238
  13.2 0.7 and_convert_fusion
  14.0 0.7 clamp_multiply_fusion
  14.7 0.8 bitcast_multiply_fusion
  15.6 0.8 bitcast_multiply_fusion.5
  17.4 0.7 copy.120
  18.0 0.7 copy.119
  18.7 171.4 %scatter_custom_fusion.1 = f32[393216]{0:T(1024)S(1)} fusion(s32[32768]{0:T(1024)S(1)} %bitcast.216, f32[32768]{0:T(1024)S(1)} %bitcast.230, f32[]{:T(128)} %constant.245.clone.1), kind=kCustom, calls=%fused_computation.75 | custom fusion | flops 32768 | bytes 1572868 | tf_op jit(solution)/shard_map/scatter-add | solution.py:87
  190.1 175.3 %scatter_fusion.1 = f32[393216]{0:T(1024)S(1)} fusion(f32[393216]{0:T(1024)S(1)} %scatter_custom_fusion.1, s32[32768]{0:T(1024)S(1)} %bitcast.209, f32[32768]{0:T(1024)S(1)} %bitcast.213), kind=kCustom, calls=%fused_computation.8 | custom fusion | flops 32768 | bytes 524288 | tf_op jit(solution)/shard_map/scatter-add | solution.py:87
  365.4 175.3 %scatter_fusion.2 = f32[393216]{0:T(1024)S(1)} fusion(f32[393216]{0:T(1024)S(1)} %scatter_fusion.1, s32[32768]{0:T(1024)S(1)} %bitcast.211, f32[32768]{0:T(1024)S(1)} %bitcast.214), kind=kCustom, calls=%fused_computation.9 | custom fusion | flops 32768 | bytes 524288 | tf_op jit(solution)/shard_map/scatter-add | solution.py:87
  540.7 175.3 %scatter_fusion.3 = f32[393216]{0:T(1024)S(1)} fusion(f32[393216]{0:T(1024)S(1)} %scatter_fusion.2, s32[32768]{0:T(1024)S(1)} %bitcast.207, f32[32768]{0:T(1024)S(1)} %bitcast.215), kind=kCustom, calls=%fused_computation.10 | custom fusion | flops 32768 | bytes 524288 | tf_op jit(solution)/shard_map/scatter-add | solution.py:87
  716.1 1.1 slice.271
  717.4 0.7 broadcast_clamp_fusion.1
  719.0 15.4 collective-permute-done.2
  734.4 1.8 fusion.62
  736.2 1.8 fusion.105
  738.0 1.8 convolution_negate_fusion
  739.8 1.8 fusion.103
  741.6 1.8 fusion.27
  743.5 1.8 fusion.26
  745.5 2.8 copy.89
  748.3 4.8 all-to-all-start
  753.1 0.7 broadcast_clamp_fusion.3
  753.7 0.7 broadcast_clamp_fusion
  754.4 23.5 %all-to-all-done = f32[2,3,256,256]{3,0,1,2:T(2,128)S(1)} async-done(((f32[2,3,256,256]{3,0,1,2:T(2,128)}), f32[2,3,256,256]{3,0,1,2:T(2,128)S(1)}, u32[]{:S(2)}, u32[]{:S(2)}) %all-to-all-start) | async-done | bytes 1572896 | tf_op jit(solution)/shard_map/all_to_all | solution.py:195
  777.9 0.8 copy.133
  779.3 3.7 fusion.34
  782.9 3.7 fusion.30
  786.6 3.9 fusion.25
  790.5 3.6 fusion.46
  794.2 3.7 fusion.24
  797.9 3.6 fusion.44
  801.5 3.9 fusion.23
  805.4 3.7 fusion.22
  809.2 2.4 copy.101
  811.6 4.8 all-to-all-start.1
  816.4 0.9 pad_maximum_fusion.3
  817.3 1.0 scatter-add.46
  818.3 22.9 %all-to-all-done.1 = f32[2,384,2,256]{3,2,0,1:T(2,128)S(1)} async-done(((f32[2,384,2,256]{3,2,0,1:T(2,128)}), f32[2,384,2,256]{3,2,0,1:T(2,128)S(1)}, u32[]{:S(2)}, u32[]{:S(2)}) %all-to-all-start.1) | async-done | bytes 1572896 | tf_op jit(solution)/shard_map/all_to_all | solution.py:203
  843.1 2.7 fusion.97
  846.7 1.8 fusion.101
  848.5 1.8 fusion.20
  850.4 1.8 fusion.21
  852.2 1.9 fusion.99
  854.2 1.8 fusion.19
  855.9 1.4 collective-permute-start.3
  857.4 5.7 while.15
  857.5 0.6 gather_fusion
  858.1 0.6 gather_fusion.1
  858.7 0.7 compare_convert_fusion.3
  859.5 2.4 fusion.260
  861.9 1.1 scatter_fusion
  863.1 3.8 collective-permute-done.3
  867.1 0.8 copy.121
  868.0 180.5 %gather_fusion.4 = f32[32768]{0:T(1024)S(1)} fusion(f32[393216]{0:T(1024)S(1)} %bitcast.194, s32[32768]{0:T(1024)S(1)} %copy-done.14), kind=kCustom, calls=%fused_computation.4 | custom fusion | bytes 393216 | tf_op jit(solution)/shard_map/gather | solution.py:98
  1048.8 180.5 %gather_fusion.3 = f32[32768]{0:T(1024)S(1)} fusion(f32[393216]{0:T(1024)S(1)} %bitcast.195, s32[32768]{0:T(1024)S(1)} %broadcast_clamp_fusion.2), kind=kCustom, calls=%fused_computation.3 | custom fusion | bytes 393216 | tf_op jit(solution)/shard_map/gather | solution.py:98
  1229.4 180.5 %gather_fusion.2 = f32[32768]{0:T(1024)S(1)} fusion(f32[393216]{0:T(1024)S(1)} %bitcast.196, s32[32768]{0:T(1024)S(1)} %copy-done.16), kind=kCustom, calls=%fused_computation.2 | custom fusion | bytes 393216 | tf_op jit(solution)/shard_map/gather | solution.py:98
  1410.2 180.5 %gather_fusion.5 = f32[32768]{0:T(1024)S(1)} fusion(f32[393216]{0:T(1024)S(1)} %bitcast.197, s32[32768]{0:T(1024)S(1)} %copy-done.15), kind=kCustom, calls=%fused_computation.5 | custom fusion | bytes 393216 | tf_op jit(solution)/shard_map/gather | solution.py:98
  1591.4 0.6 maximum_add_fusion
  (158 shorter events, 6.3 us)
Async XLA Ops:
  0.0 16.8 %copy-start.54 = (s32[2048]{0:T(1024)S(1)}, s32[2048]{0:T(1024)}, u32[]{:S(2)}) copy-start(s32[2048]{0:T(1024)} %param.24) | copy-start | bytes 24580
  0.0 16.9 %copy-start.55 = (s32[2048]{0:T(1024)S(1)}, s32[2048]{0:T(1024)}, u32[]{:S(2)}) copy-start(s32[2048]{0:T(1024)} %param.25) | copy-start | bytes 24580
  1.4 814.9 %collective-permute-start = (f32[6,2048]{1,0:T(8,128)}, f32[6,2048]{1,0:T(8,128)}, u32[]{:S(2)}, u32[]{:S(2)}) collective-permute-start(f32[6,2048]{1,0:T(8,128)} %pad_maximum_fusion.4), channel_id=1, source_target_pairs={{0,1},{1,2},{2,3},{3,4},{4,5},{5,6},{6,7},{7,8},{8,9},{9,10},{10,1... | collective-permute-start | bytes 147464 | tf_op jit(solution)/shard_map/ppermute | solution.py:29
  1.4 814.9 %collective-permute-start.1 = (f32[6,2048]{1,0:T(8,128)}, f32[6,2048]{1,0:T(8,128)}, u32[]{:S(2)}, u32[]{:S(2)}) collective-permute-start(f32[6,2048]{1,0:T(8,128)} %pad_maximum_fusion.4), channel_id=1, source_target_pairs={{1,0},{2,1},{3,2},{4,3},{5,4},{6,5},{7,6},{8,7},{9,8},{10,9},{11,1... | collective-permute-start | bytes 147464 | tf_op jit(solution)/shard_map/ppermute | solution.py:30
  12.3 4.8 copy-start.7
  12.3 4.8 copy-start.9
  14.0 3.2 copy-start.43
  14.0 3.2 copy-start.45
  14.0 3.2 copy-start.47
  14.0 3.2 copy-start.49
  15.5 1.7 copy-start.17
  15.5 1.7 copy-start.23
  15.5 1.7 copy-start.25
  15.5 1.7 copy-start.27
  16.4 0.9 copy-start.19
  16.4 0.9 copy-start.21
  16.4 0.9 copy-start.29
  16.4 0.9 copy-start.31
  16.4 0.9 copy-start.33
  16.4 0.9 copy-start.35
  16.5 0.9 copy-start.37
  16.5 0.9 copy-start.39
  17.2 348.1 %copy-start.12 = (s32[4,16,4,128]{3,1,2,0:T(8,128)}, s32[4,16,4,128]{3,1,2,0:T(8,128)S(1)}, u32[]{:S(2)}) copy-start(s32[4,16,4,128]{3,1,2,0:T(8,128)S(1)} %copy.113) | copy-start | bytes 393220
  17.3 348.0 %copy-start.5 = (s32[4,16,4,128]{3,1,2,0:T(8,128)}, s32[4,16,4,128]{3,1,2,0:T(8,128)S(1)}, u32[]{:S(2)}) copy-start(s32[4,16,4,128]{3,1,2,0:T(8,128)S(1)} %copy.115) | copy-start | bytes 393220
  365.4 175.3 %copy-start.4 = (s32[4,16,4,128]{3,1,2,0:T(8,128)S(1)}, s32[4,16,4,128]{3,1,2,0:T(8,128)}, u32[]{:S(2)}) copy-start(s32[4,16,4,128]{3,1,2,0:T(8,128)} %copy.119) | copy-start | bytes 393220
  365.4 175.3 %copy-start.11 = (f32[4,16,4,128]{3,1,2,0:T(8,128)S(1)}, f32[4,16,4,128]{3,1,2,0:T(8,128)}, u32[]{:S(2)}) copy-start(f32[4,16,4,128]{3,1,2,0:T(8,128)} %copy.120) | copy-start | bytes 393220
  716.1 2.9 copy-start.6
  717.2 17.2 %collective-permute-start.2 = (f32[3,256,256]{2,1,0:T(8,128)}, f32[3,256,256]{2,1,0:T(8,128)S(1)}, u32[]{:S(2)}, u32[]{:S(2)}) collective-permute-start(f32[3,256,256]{2,1,0:T(8,128)} %slice.271), channel_id=1, source_target_pairs={{0,1},{1,2},{2,3},{3,4},{4,5},{5,6},{6,7},{7,8},{8,9},{9,10},{10,1... | collective-permute-start | bytes 2359304 | tf_op jit(solution)/shard_map/ppermute | solution.py:38
  748.3 4.8 copy-start.13
  748.3 29.6 %all-to-all-start = ((f32[2,3,256,256]{3,0,1,2:T(2,128)}), f32[2,3,256,256]{3,0,1,2:T(2,128)S(1)}, u32[]{:S(2)}, u32[]{:S(2)}) async-start(f32[2,3,256,256]{3,0,1,2:T(2,128)} %copy.89), calls=%async_computation | async-start | bytes 3145728 | tf_op jit(solution)/shard_map/all_to_all | solution.py:195
  779.3 7.3 copy-start.1
  811.6 4.8 copy-start.41
  811.6 4.8 copy-start.42
  811.6 5.7 copy-start.53
  811.6 29.6 %all-to-all-start.1 = ((f32[2,384,2,256]{3,2,0,1:T(2,128)}), f32[2,384,2,256]{3,2,0,1:T(2,128)S(1)}, u32[]{:S(2)}, u32[]{:S(2)}) async-start(f32[2,384,2,256]{3,2,0,1:T(2,128)} %copy.101), calls=%async_computation.1 | async-start | bytes 3145728 | tf_op jit(solution)/shard_map/all_to_all | solution.py:203
  846.1 2.4 copy-start
  854.1 3.2 copy-start.51
  854.1 3.2 copy-start.52
  855.9 10.9 collective-permute-start.3
  863.0 4.0 copy-start.2
  867.0 0.9 copy-start.14
  868.0 180.6 %copy-start.8 = (f32[4,2048]{1,0:T(4,128)S(1)}, f32[4,2048]{1,0:T(4,128)}, u32[]{:S(2)}) copy-start(f32[4,2048]{1,0:T(4,128)} %copy-done.7) | copy-start | bytes 98308
  868.0 180.6 %copy-start.10 = (f32[4,2048]{1,0:T(4,128)S(1)}, f32[4,2048]{1,0:T(4,128)}, u32[]{:S(2)}) copy-start(f32[4,2048]{1,0:T(4,128)} %copy-done.9) | copy-start | bytes 98308
  868.0 180.7 %copy-start.18 = (f32[4,2048]{1,0:T(4,128)S(1)}, f32[4,2048]{1,0:T(4,128)}, u32[]{:S(2)}) copy-start(f32[4,2048]{1,0:T(4,128)} %copy-done.17) | copy-start | bytes 98308
  868.0 180.7 %copy-start.20 = (f32[4,2048]{1,0:T(4,128)S(1)}, f32[4,2048]{1,0:T(4,128)}, u32[]{:S(2)}) copy-start(f32[4,2048]{1,0:T(4,128)} %copy-done.19) | copy-start | bytes 98308
  868.0 180.7 %copy-start.22 = (f32[4,2048]{1,0:T(4,128)S(1)}, f32[4,2048]{1,0:T(4,128)}, u32[]{:S(2)}) copy-start(f32[4,2048]{1,0:T(4,128)} %copy-done.21) | copy-start | bytes 98308
  868.0 180.7 %copy-start.44 = (f32[2048]{0:T(1024)S(1)}, f32[2048]{0:T(1024)}, u32[]{:S(2)}) copy-start(f32[2048]{0:T(1024)} %copy-done.43) | copy-start | bytes 24580
  1048.8 180.6 %copy-start.16 = (s32[32768]{0:T(1024)S(1)}, s32[32768]{0:T(1024)}, u32[]{:S(2)}) copy-start(s32[32768]{0:T(1024)} %broadcast_clamp_fusion.3) | copy-start | bytes 393220
  1229.4 180.6 %copy-start.15 = (s32[32768]{0:T(1024)S(1)}, s32[32768]{0:T(1024)}, u32[]{:S(2)}) copy-start(s32[32768]{0:T(1024)} %broadcast_clamp_fusion) | copy-start | bytes 393220
  1410.1 180.7 %copy-start.24 = (f32[4,2048]{1,0:T(4,128)S(1)}, f32[4,2048]{1,0:T(4,128)}, u32[]{:S(2)}) copy-start(f32[4,2048]{1,0:T(4,128)} %copy-done.23) | copy-start | bytes 98308
  1410.1 180.7 %copy-start.26 = (f32[4,2048]{1,0:T(4,128)S(1)}, f32[4,2048]{1,0:T(4,128)}, u32[]{:S(2)}) copy-start(f32[4,2048]{1,0:T(4,128)} %copy-done.25) | copy-start | bytes 98308
  1410.1 180.7 %copy-start.28 = (f32[4,2048]{1,0:T(4,128)S(1)}, f32[4,2048]{1,0:T(4,128)}, u32[]{:S(2)}) copy-start(f32[4,2048]{1,0:T(4,128)} %copy-done.27) | copy-start | bytes 98308
  1410.1 180.7 %copy-start.30 = (f32[4,2048]{1,0:T(4,128)S(1)}, f32[4,2048]{1,0:T(4,128)}, u32[]{:S(2)}) copy-start(f32[4,2048]{1,0:T(4,128)} %copy-done.29) | copy-start | bytes 98308
  1410.1 180.7 %copy-start.32 = (f32[4,2048]{1,0:T(4,128)S(1)}, f32[4,2048]{1,0:T(4,128)}, u32[]{:S(2)}) copy-start(f32[4,2048]{1,0:T(4,128)} %copy-done.31) | copy-start | bytes 98308
  1410.1 180.7 %copy-start.34 = (f32[4,2048]{1,0:T(4,128)S(1)}, f32[4,2048]{1,0:T(4,128)}, u32[]{:S(2)}) copy-start(f32[4,2048]{1,0:T(4,128)} %copy-done.33) | copy-start | bytes 98308
  1410.1 180.7 %copy-start.36 = (f32[4,2048]{1,0:T(4,128)S(1)}, f32[4,2048]{1,0:T(4,128)}, u32[]{:S(2)}) copy-start(f32[4,2048]{1,0:T(4,128)} %copy-done.35) | copy-start | bytes 98308
  1410.1 180.7 %copy-start.38 = (f32[4,2048]{1,0:T(4,128)S(1)}, f32[4,2048]{1,0:T(4,128)}, u32[]{:S(2)}) copy-start(f32[4,2048]{1,0:T(4,128)} %copy-done.37) | copy-start | bytes 98308
  1410.1 180.7 %copy-start.40 = (f32[4,2048]{1,0:T(4,128)S(1)}, f32[4,2048]{1,0:T(4,128)}, u32[]{:S(2)}) copy-start(f32[4,2048]{1,0:T(4,128)} %copy-done.39) | copy-start | bytes 98308
  1410.1 180.7 %copy-start.46 = (f32[2048]{0:T(1024)S(1)}, f32[2048]{0:T(1024)}, u32[]{:S(2)}) copy-start(f32[2048]{0:T(1024)} %copy-done.45) | copy-start | bytes 24580
  1410.2 180.7 %copy-start.48 = (f32[2048]{0:T(1024)S(1)}, f32[2048]{0:T(1024)}, u32[]{:S(2)}) copy-start(f32[2048]{0:T(1024)} %copy-done.47) | copy-start | bytes 24580
  1410.2 180.7 %copy-start.50 = (f32[2048]{0:T(1024)S(1)}, f32[2048]{0:T(1024)}, u32[]{:S(2)}) copy-start(f32[2048]{0:T(1024)} %copy-done.49) | copy-start | bytes 24580
  1410.2 181.3 %copy-start.3 = (f32[16,3,128]{2,1,0:T(4,128)S(1)}, f32[16,3,128]{2,1,0:T(4,128)}, u32[]{:S(2)}) copy-start(f32[16,3,128]{2,1,0:T(4,128)} %copy-done.2) | copy-start | bytes 73732
where the time goes:
time: 1600 us; the launch traced here: 1590 us
  local copies, waits for them, and re-layouts  741 us (46%)
  other arithmetic  711 us (44%)
  waiting for transfers between devices  65.6 us (4%)
  matrix products  52.4 us (3%)
  starting transfers between devices  19.3 us (1%)
    gather x8, local copies, waits for them, and re-layouts, sample_from(): sampled = flat_potential[cells] * valid[None, None, :]  722 us
    scatter-add x4, other arithmetic, spread_into(): grid = grid.at[cells].add(amount)  697 us
  transfers between devices with their start and end apart: 6, of which 4 were waited for; matrix products, arithmetic and copies ran while one was open for 48% of the time, Pallas kernels for 0%

commit v1 on v0

v1 whole, which is shorter than its diff:
```python
import functools

import jax
import jax.numpy as jnp
import numpy as np
from jax import lax
from jax.experimental import pallas as pl
from jax.experimental.pallas import tpu as pltpu
from jax.sharding import PartitionSpec as P

CL = 128
CLU_DEV = 16
GX = 384
GY = 256
GZ = 256
DEV = 128
ATOM_DEV = 2048
SLOTS = 32
CHUNK = 512
AXES = ("grp", "sp")

f32, bf16 = jnp.float32, jnp.bfloat16
VM = pl.BlockSpec(memory_space=pltpu.VMEM)
SM = pl.BlockSpec(memory_space=pltpu.SMEM)


def halves(table):
    high = table.astype(bf16)
    low = (table - high.astype(np.float64)).astype(bf16)
    return high, low


@functools.cache
def tables():
    d = np.arange(128)[:, None]
    y = np.arange(GY)[None, :]
    angle = 2 * np.pi * ((d * y) % GY) / GY
    real, imag = np.cos(angle), -np.sin(angle)
    imag[0] = 1 - 2 * (np.arange(GY) % 2)
    forward_y = np.concatenate([real, imag], 0)
    scale = np.full((1, 256), 2.0)
    scale[0, 0] = scale[0, 128] = 1.0
    backward_y = forward_y.T * scale / (GX * GY * GZ)
    z = np.arange(GZ)
    angle = 2 * np.pi * ((z[:, None] * z[None, :]) % GZ) / GZ
    cos, sin = np.cos(angle), np.sin(angle)
    forward_z = np.block([[cos, -sin], [sin, cos]])
    backward_z = np.block([[cos, sin], [-sin, cos]])
    k = np.arange(GX)
    forward_x = []
    for p in range(3):
        angle = 2 * np.pi * ((k[:, None] * (3 * np.arange(128)[None, :] + p)) % GX) / GX
        forward_x += [np.cos(angle), np.sin(angle)]
    backward_x = np.concatenate(
        [np.concatenate([forward_x[2 * p].T, forward_x[2 * p + 1].T], 1) for p in range(3)], 0
    )
    forward_x = np.concatenate(forward_x, 1)
    out = []
    for table in (forward_y, forward_x, forward_z, backward_z, backward_x, backward_y):
        out += list(halves(table))
    return out


def split(x):
    high = x.astype(bf16)
    return high, (x - high.astype(f32)).astype(bf16)


def nn(a, b):
    return lax.dot_general(a, b, (((1,), (0,)), ((), ())), preferred_element_type=f32)


def nt(a, b):
    return lax.dot_general(a, b, (((1,), (1,)), ((), ())), preferred_element_type=f32)


def left(table_high, table_low, x):
    high, low = split(x)
    return nn(
        jnp.concatenate([table_high, table_high, table_low], 1),
        jnp.concatenate([high, low, high], 0),
    )


def right(x, table_high, table_low):
    high, low = split(x)
    return nn(
        jnp.concatenate([high, low, high], 1),
        jnp.concatenate([table_high, table_high, table_low], 0),
    )


def dense(base, weights):
    n = base.shape[1]
    step = (lax.broadcasted_iota(jnp.int32, (256, n), 0) - base) & 255
    at = [step == k for k in range(4)]
    out = []
    for w in weights:
        r = jnp.where(at[3], w[3], 0.0)
        for k in (2, 1, 0):
            r = jnp.where(at[k], w[k], r)
        out.append(r)
    return out


def atoms(ref, start, n):
    cols = pl.ds(pl.multiple_of(start, n), n)
    g = lambda r: ref[r : r + 1, cols]
    code, column = g(30).astype(jnp.int32), g(31).astype(jnp.int32)
    moment = [g(3 + i) for i in range(3)]
    v = [[g(6 + 4 * i + k) for k in range(4)] for i in range(3)]
    s = [[g(18 + 4 * i + k) for k in range(4)] for i in range(3)]
    return code & 255, column, code >> 8, moment, v, s


def plane_weights(local, w, shift):
    out = []
    for p in range(3):
        step = p + shift - local
        r = jnp.zeros_like(w[0])
        for k in range(4):
            r = jnp.where(step == k, w[k], r)
        out.append(r)
    return out


def spread_chunk(ref, start, shift, grid):
    row, column, local, m, v, s = atoms(ref, start, CHUNK)
    v2, s2 = dense(column, [v[2], s[2]])
    v1, s1 = dense(row, [v[1], s[1]])
    x0 = plane_weights(local, v[0], shift)
    xs = plane_weights(local, s[0], shift)
    a = jnp.concatenate([v1 * (m[0] * xs[p]) + s1 * (m[1] * x0[p]) for p in range(3)], 0)
    b = jnp.concatenate([v1 * (m[2] * x0[p]) for p in range(3)], 0)
    ah, al = split(a)
    bh, bl = split(b)
    vh, vl = split(v2)
    sh, sl = split(s2)
    grid[...] += nt(
        jnp.concatenate([ah, bh, ah, al, bh, bl], 1), jnp.concatenate([vh, sh, vl, vh, sl, sh], 1)
    )


def spread_kernel(own, before, grid):
    grid[...] = jnp.zeros_like(grid)

    def body(i, c):
        spread_chunk(own, i * CHUNK, 0, grid)
        spread_chunk(before, i * CHUNK, 3, grid)
        return c

    lax.fori_loop(0, ATOM_DEV // CHUNK, body, 0)


def sample_chunk(ref, start, shift, stacked, out):
    row, column, local, m, v, s = atoms(ref, start, CHUNK)
    v2, s2 = dense(column, [v[2], s[2]])
    v1, s1 = dense(row, [v[1], s[1]])
    x0 = plane_weights(local, v[0], shift)
    xs = plane_weights(local, s[0], shift)
    vh, vl = split(v2)
    sh, sl = split(s2)
    pot = stacked[...]
    tv = nn(pot, jnp.concatenate([vh, vl, vh], 0))
    ts = nn(pot, jnp.concatenate([sh, sl, sh], 0))
    tv = [tv[p * 256 : p * 256 + 256] for p in range(3)]
    ts = [ts[p * 256 : p * 256 + 256] for p in range(3)]
    ax = tv[0] * xs[0] + tv[1] * xs[1] + tv[2] * xs[2]
    ay = tv[0] * x0[0] + tv[1] * x0[1] + tv[2] * x0[2]
    az = ts[0] * x0[0] + ts[1] * x0[1] + ts[2] * x0[2]
    r = [jnp.sum(w * t, 0, keepdims=True) for w, t in ((v1, ax), (s1, ay), (v1, az))]
    out[:, pl.ds(pl.multiple_of(start, CHUNK), CHUNK)] = -jnp.concatenate(r, 0)


def sample_kernel(own, before, pot, out_own, out_before, stacked):
    high, low = split(pot[...])
    stacked[:, 0:256] = high
    stacked[:, 256:512] = high
    stacked[:, 512:768] = low

    def body(i, c):
        sample_chunk(before, i * CHUNK, 3, stacked, out_before)
        sample_chunk(own, i * CHUNK, 0, stacked, out_own)
        return c

    lax.fori_loop(0, ATOM_DEV // CHUNK, body, 0)


def direct_kernel(home, other, count, own, before, after, out, ext, acc):
    for part, ref in enumerate((before, own, after)):
        shift = 2.0 * (part - 1)
        for c in range(CLU_DEV):
            x = ref[0:8, c * CL : (c + 1) * CL]
            if part != 1:
                x = x + jnp.where(lax.broadcasted_iota(jnp.int32, (8, CL), 0) == 0, shift, 0.0)
            ext[part * CLU_DEV + c] = x
    acc[...] = jnp.zeros_like(acc)
    eye = (
        lax.broadcasted_iota(jnp.int32, (CL, CL), 0) == lax.broadcasted_iota(jnp.int32, (CL, CL), 1)
    ).astype(f32)
    which = lax.broadcasted_iota(jnp.int32, (CLU_DEV, 8, CL), 0)

    def slot(t, carry):
        h, o = home[t], other[t]
        hx = ext[h + CLU_DEV]
        ox = ext[o].T
        delta = [hx[a : a + 1, :] - ox[:, a : a + 1] for a in range(3)]
        m = [ox[:, 3 + a : 4 + a] for a in range(3)]
        q = delta[0] * delta[0] + delta[1] * delta[1] + delta[2] * delta[2]
        inverse = lax.rsqrt(q + 0.25)
        square = inverse * inverse
        self_slot = jnp.where(o == h + CLU_DEV, 1.0, 0.0)
        first = jnp.exp(-0.5 * q) * (inverse * square) * (1.0 - self_slot * eye)
        second = 3.0 * first * square
        along = second * (delta[0] * m[0] + delta[1] * m[1] + delta[2] * m[2])
        e = [jnp.sum(along * delta[a] - first * m[a], 0, keepdims=True) for a in range(3)]
        live = jnp.where(t < count[0], 0.125, 0.0)
        e = jnp.concatenate(e + [jnp.zeros((5, CL), f32)], 0) * live
        acc[...] += jnp.where(which == h, e[None], 0.0)
        return carry

    lax.fori_loop(0, SLOTS, slot, 0)
    for c in range(CLU_DEV):
        out[:, c * CL : (c + 1) * CL] = acc[c][0:3]


def device_id(t):
    return (t // 64, lax.rem(t, 64))


def exchange_start(me, p, src, dst, send_sem, recv_sem):
    def send(i, c):
        t = lax.rem(me + i, DEV)
        pltpu.make_async_remote_copy(
            src_ref=src.at[p, t],
            dst_ref=dst.at[p, me],
            send_sem=send_sem.at[p],
            recv_sem=recv_sem.at[p],
            device_id=device_id(t),
            device_id_type=pl.DeviceIdType.MESH,
        ).start()
        return c

    lax.fori_loop(1, DEV, send, 0)
    dst[p, pl.ds(me, 1)] = src[p, pl.ds(me, 1)]


def exchange_wait(p, src, sem):
    part = src.at[p, pl.ds(0, DEV - 1)]
    pltpu.make_async_copy(part, part, sem.at[p]).wait()


def to_rows(ref, p, value):
    view = ref.at[p].reshape(512, 128)
    for c in range(2):
        for h in range(2):
            view[pl.ds(2 * c + h, 128, stride=4), :] = value[
                c * 128 : c * 128 + 128, h * 128 : h * 128 + 128
            ]


def from_rows(ref, p):
    view = ref.at[p].reshape(512, 128)
    part = [view[pl.ds(k, 128, stride=4), :] for k in range(4)]
    return jnp.concatenate(part[0:2], 1), jnp.concatenate(part[2:4], 1)


def mesh_kernel(
    grid, keep, turn, fyh, fyl, fxh, fxl, fzh, fzl, bzh, bzl, bxh, bxl, byh, byl, pot,
    send1, recv1, send2, recv2, spec, ss1, rs1, ss2, rs2,
):
    me = lax.axis_index("grp") * 64 + lax.axis_index("sp")
    barrier = pltpu.get_barrier_semaphore()

    def greet(i, c):
        pl.semaphore_signal(
            barrier, inc=1, device_id=device_id(lax.rem(me + i, DEV)), device_id_type=pl.DeviceIdType.MESH
        )
        return c

    lax.fori_loop(1, DEV, greet, 0)
    pl.semaphore_wait(barrier, DEV - 1)
    for p in range(3):
        to_rows(send1, p, left(fyh[...], fyl[...], grid[p * 256 : p * 256 + 256, :]))
        exchange_start(me, p, send1, recv1, ss1, rs1)

    def forward(sign):
        total = jnp.zeros((GX, 512), f32)
        for p in range(3):
            real, imag = from_rows(recv1, p)
            imag = imag * sign
            x = jnp.concatenate(
                [jnp.concatenate([real, imag], 1), jnp.concatenate([imag, -real], 1)], 0
            )
            cols = slice(p * 256, p * 256 + 256)
            total = total + left(fxh[:, cols], fxl[:, cols], x)
        return right(total, fzh[...], fzl[...])

    for p in range(3):
        exchange_wait(p, recv1, rs1)
    spec[...] = forward(1.0) * jnp.concatenate([keep[...], keep[...]], 1)

    @pl.when(me == 0)
    def _():
        spec[...] += forward(-1.0) * jnp.concatenate([turn[...], turn[...]], 1)

    back = right(spec[...], bzh[...], bzl[...])
    real, imag = back[:, 0:256], back[:, 256:512]
    x = jnp.concatenate([jnp.concatenate([real, imag], 1), jnp.concatenate([-imag, real], 1)], 0)
    high, low = split(x)
    x = jnp.concatenate([high, low, high], 0)
    for p in range(3):
        rows = slice(p * 128, p * 128 + 128)
        y = nn(jnp.concatenate([bxh[rows, :], bxh[rows, :], bxl[rows, :]], 1), x)
        to_rows(send2, p, jnp.concatenate([y[:, 0:256], y[:, 256:512]], 0))
        exchange_start(me, p, send2, recv2, ss2, rs2)
    for p in range(3):
        exchange_wait(p, recv2, rs2)
        real, imag = from_rows(recv2, p)
        pot[p * 256 : p * 256 + 256, :] = left(byh[...], byl[...], jnp.concatenate([real, imag], 0))
    for p in range(3):
        exchange_wait(p, send1, ss1)
        exchange_wait(p, send2, ss2)


def negated(x):
    return jnp.roll(x[::-1, ::-1], (1, 1), (0, 1))


def on_device(
    positions,
    dipoles,
    spline_values,
    spline_slopes,
    plane_base,
    row_base,
    column_base,
    pair_home,
    pair_other,
    pair_count,
    influence,
):
    up = [(i, (i + 1) % DEV) for i in range(DEV)]
    down = [(j, i) for i, j in up]
    me = lax.axis_index("grp") * 64 + lax.axis_index("sp")
    near = jnp.concatenate([positions, dipoles], axis=0)
    local = plane_base % 3
    own = jnp.concatenate(
        [
            near,
            spline_values.reshape(12, ATOM_DEV),
            spline_slopes.reshape(12, ATOM_DEV),
            (row_base + 256 * local).astype(f32)[None],
            column_base.astype(f32)[None],
        ],
        axis=0,
    )
    before = lax.ppermute(own, AXES, up)
    after = lax.ppermute(near, AXES, down)
    row0, row1 = influence[:, 0, :], influence[:, 1, :]
    lower = me < 64
    sent1 = lax.ppermute(
        jnp.where(lower, row0, row1), AXES, [(e, 2 * e if e < 64 else 255 - 2 * e) for e in range(DEV)]
    )
    sent2 = lax.ppermute(
        jnp.where(lower, row1, row0),
        AXES,
        [(e, 2 * e + 1 if e < 64 else (256 - 2 * e) % DEV) for e in range(DEV)],
    )
    even = me % 2 == 0
    u, v = jnp.where(even, sent1, sent2), jnp.where(even, sent2, sent1)
    nu, nv = negated(u), negated(v)
    first = me == 0
    keep = jnp.where(first, 0.25 * ((u + nu) + (v + nv)), 0.5 * (u + nv))
    turn = jnp.where(first, 0.25 * ((u + nu) - (v + nv)), 0.0)
    limit = pltpu.CompilerParams(vmem_limit_bytes=50 << 20)
    grid = pl.pallas_call(
        spread_kernel,
        out_shape=jax.ShapeDtypeStruct((768, 256), f32),
        in_specs=[VM] * 2,
        out_specs=VM,
        compiler_params=limit,
        name="spread",
    )(own, before)
    pot = pl.pallas_call(
        mesh_kernel,
        out_shape=jax.ShapeDtypeStruct((768, 256), f32),
        in_specs=[VM] * 15,
        out_specs=VM,
        scratch_shapes=[pltpu.VMEM((3, DEV, 4, 128), f32)] * 4
        + [pltpu.VMEM((GX, 512), f32)]
        + [pltpu.SemaphoreType.DMA((3,))] * 4,
        compiler_params=pltpu.CompilerParams(
            vmem_limit_bytes=50 << 20, collective_id=0, has_side_effects=True
        ),
        name="reciprocal",
    )(grid, keep, turn, *[jnp.asarray(t) for t in tables()])
    out_own, out_before = pl.pallas_call(
        sample_kernel,
        out_shape=[jax.ShapeDtypeStruct((3, ATOM_DEV), f32)] * 2,
        in_specs=[VM] * 3,
        out_specs=[VM] * 2,
        scratch_shapes=[pltpu.VMEM((768, 768), bf16)],
        compiler_params=limit,
        name="sample",
    )(own, before, pot)
    direct = pl.pallas_call(
        direct_kernel,
        out_shape=jax.ShapeDtypeStruct((3, ATOM_DEV), f32),
        in_specs=[SM] * 3 + [VM] * 3,
        out_specs=VM,
        scratch_shapes=[pltpu.VMEM((48, 8, CL), f32), pltpu.VMEM((CLU_DEV, 8, CL), f32)],
        compiler_params=limit,
        name="direct",
    )(pair_home, pair_other, pair_count, own, before, jnp.concatenate([after, after[:2]], 0))
    return direct + out_own + lax.ppermute(out_before, AXES, down)


def solution(mesh):
    placed = (
        P(None, AXES),
        P(None, AXES),
        P(None, None, AXES),
        P(None, None, AXES),
        P(AXES),
        P(AXES),
        P(AXES),
        P(AXES),
        P(AXES),
        P(AXES),
        P(None, AXES, None),
    )
    return jax.shard_map(
        on_device, mesh=mesh, in_specs=placed, out_specs=P(None, AXES), check_vma=False
    )
```

time: 1600 us -> 125 us (0.08)
  local copies, waits for them, and re-layouts: 741 us -> 9.95 us
  other arithmetic: 711 us -> 1.27 us
  Pallas kernels: 0 us -> 78.2 us
  matrix products: 52.4 us -> 0 us
  waiting for transfers between devices: 65.6 us -> 16.2 us
    gather x10 -> x0, local copies, waits for them, and re-layouts: 723 us -> none  [the longest x8 722 us: sample_from(): sampled = flat_potential[cells] * valid[None, None, :]]
    scatter-add x5 -> x0, other arithmetic: 698 us -> none  [the longest x4 697 us: spread_into(): grid = grid.at[cells].add(amount)]
    pallas_call x0 -> x4, Pallas kernels: none -> 78.2 us  [the longest x1 38.5 us: on_device(): pl.pallas_call(mesh_kernel, out_shape=jax.ShapeDtypeStruct((768, 256), f3...]
    dot_general x20 -> x0, matrix products: 52.4 us -> none  [the longest x8 15.5 us: along_y(): return jnp.einsum('pyz,ky->pkz', field, table, precision=highest)]
    all_to_all x2 -> x0, waiting for transfers between devices: 46.4 us -> none  [the longest x1 23.5 us: on_device(): lax.all_to_all(planes_grid, ('grp', 'sp'), split_axis=2, concat_axis=1, t...]
  transfers between devices with their start and end apart: 6 -> 5, of which waited for: 4 -> 2; matrix products, arithmetic and copies ran while one was open for 48% -> 0% of each run, Pallas kernels for 0% -> 21%
where the time goes in v1:
time: 125 us; the launch traced here: 124 us
  Pallas kernels  78.2 us (63%)
  starting transfers between devices  17.6 us (14%)
  waiting for transfers between devices  16.2 us (13%)
  local copies, waits for them, and re-layouts  9.95 us (8%)
  other arithmetic  1.27 us (1%)
    pallas_call x1, Pallas kernels, on_device(): pl.pallas_call(mesh_kernel, out_shape=jax.ShapeDtypeStruct((768, 256), f3...  38.5 us
    ppermute x1, waiting for transfers between devices, on_device(): before = lax.ppermute(own, AXES, up)  14.9 us
    pallas_call x1, Pallas kernels, on_device(): pl.pallas_call(spread_kernel, out_shape=jax.ShapeDtypeStruct((768, 256),...  14.7 us
    pallas_call x1, Pallas kernels, on_device(): pl.pallas_call(sample_kernel, out_shape=[jax.ShapeDtypeStruct((3, ATOM_DE...  13.9 us
    pallas_call x1, Pallas kernels, on_device(): pl.pallas_call(direct_kernel, out_shape=jax.ShapeDtypeStruct((3, ATOM_DEV...  11.1 us
    ppermute x1, starting transfers between devices, on_device(): after = lax.ppermute(near, AXES, down)  6.83 us
    ppermute x1, starting transfers between devices, on_device(): return direct + out_own + lax.ppermute(out_before, AXES, down)  5.41 us
    unnamed x40, local copies, waits for them, and re-layouts  4.8 us
  transfers between devices with their start and end apart: 5, of which 2 were waited for; matrix products, arithmetic and copies ran while one was open for 0% of the time, Pallas kernels for 21%

profile of v1, /device:TPU:0, one launch (start us, length us, event | category | flops | bytes accessed | tf_op | source)
XLA Modules:
  0.0 124.2 jit_solution(12575184842798696371)
XLA Ops:
  0.0 2.1 %fusion.9 = (f32[384,1,256]{2,1,0:T(1,128)S(1)}, f32[384,1,256]{2,1,0:T(1,128)S(1)}) fusion(f32[384,2,256]{2,1,0:T(2,128)} %param.33), kind=kLoop, calls=%fused_computation.25 | loop fusion | bytes 1572864 | tf_op jit(solution)/shard_map/slice | solution.py:360
  2.1 0.0 copy-start.15
  2.1 0.1 select_bitcast_fusion
  2.2 0.7 collective-permute-start.2
  2.9 0.0 copy-start.16
  2.9 3.0 %collective-permute-start.3 = (f32[384,256]{1,0:T(8,128)S(1)}, f32[384,256]{1,0:T(8,128)S(1)}, u32[]{:S(2)}, u32[]{:S(2)}) collective-permute-start(f32[384,256]{1,0:T(8,128)S(1)} %get-tuple-element.13), channel_id=1, source_target_pairs={{0,1},{1,3},{2,5},{3,7},{4,9},{5,11},{6,13},{7,15},{8,17},{9,19},{... | collective-permute-start | bytes 1179656 | tf_op jit(solution)/shard_map/ppermute | solution.py:365
  5.9 0.0 copy-done.15
  5.9 0.0 copy-done.16
  5.9 0.0 copy-start.19
  6.0 0.0 copy-start.17
  6.0 0.0 copy-start.18
  6.0 0.0 copy-start.14
  6.0 0.6 copy-done.19
  6.6 0.0 copy-start.13
  6.7 0.0 copy-done.17
  6.7 0.0 copy-done.18
  6.7 0.1 copy-done.14
  6.8 0.7 copy-done.13
  7.4 0.4 concatenate.24.own
  7.8 1.7 %collective-permute-start = (f32[32,2048]{1,0:T(8,128)S(1)}, f32[32,2048]{1,0:T(8,128)S(1)}, u32[]{:S(2)}, u32[]{:S(2)}) collective-permute-start(f32[32,2048]{1,0:T(8,128)S(1)} %concatenate.24.own), channel_id=1, source_target_pairs={{0,1},{1,2},{2,3},{3,4},{4,5},{5,6},{6,7},{7,8},{8,9},{9,10},{10,1... | collective-permute-start | bytes 786440 | tf_op jit(solution)/shard_map/ppermute | solution.py:358
  9.6 6.8 %collective-permute-start.1 = (f32[6,2048]{1,0:T(8,128)S(1)}, f32[6,2048]{1,0:T(8,128)S(1)}, u32[]{:S(2)}, u32[]{:S(2)}) collective-permute-start(f32[6,2048]{1,0:T(8,128)S(1)} %pad_maximum_fusion.2), channel_id=1, source_target_pairs={{1,0},{2,1},{3,2},{4,3},{5,4},{6,5},{7,6},{8,7},{9,8},{10,9},{11,1... | collective-permute-start | bytes 147464 | tf_op jit(solution)/shard_map/ppermute | solution.py:359
  17.0 1.3 %collective-permute-done.1 = f32[6,2048]{1,0:T(8,128)S(1)} collective-permute-done((f32[6,2048]{1,0:T(8,128)S(1)}, f32[6,2048]{1,0:T(8,128)S(1)}, u32[]{:S(2)}, u32[]{:S(2)}) %collective-permute-start.1) | collective-permute-done | bytes 49184 | tf_op jit(solution)/shard_map/ppermute | solution.py:359
  18.3 14.9 %collective-permute-done.before = f32[32,2048]{1,0:T(8,128)S(1)} collective-permute-done((f32[32,2048]{1,0:T(8,128)S(1)}, f32[32,2048]{1,0:T(8,128)S(1)}, u32[]{:S(2)}, u32[]{:S(2)}) %collective-permute-start) | collective-permute-done | bytes 262176 | tf_op jit(solution)/shard_map/ppermute | solution.py:358
  33.2 14.7 %spread.1.grid = f32[768,256]{1,0:T(8,128)S(1)} custom-call(f32[32,2048]{1,0:T(8,128)S(1)} %concatenate.24.own, f32[32,2048]{1,0:T(8,128)S(1)} %collective-permute-done.before), custom_call_target="tpu_custom_call" | custom-call | tf_op jit(solution)/shard_map/spread/pallas_call | solution.py:377
  48.0 0.0 copy-start
  48.0 0.0 collective-permute-done.2
  48.0 0.0 collective-permute-done.3
  48.0 0.1 broadcast_select_fusion
  48.1 0.8 copy-done
  49.0 1.0 slice.55
  50.0 1.0 slice.61
  51.1 0.2 slice.53
  51.3 0.2 slice.59
  51.5 0.0 copy-start.7
  51.5 0.0 copy-start.8
  51.5 0.0 copy-start.10
  51.5 0.2 fusion.3
  51.7 0.0 copy-start.2
  51.7 0.0 copy-start.3
  51.7 0.0 copy-start.4
  51.7 0.0 copy-start.5
  51.7 0.0 copy-start.6
  51.7 0.3 multiply_select_fusion
  52.0 0.3 copy-done.7
  52.4 0.1 copy-done.8
  52.4 0.1 copy-done.9
  52.5 0.1 copy-done.10
  52.6 0.3 copy-done.2
  52.8 0.2 copy-done.3
  53.0 0.2 copy-done.4
  53.2 0.2 copy-done.5
  53.3 0.2 copy-done.6
  53.5 38.5 %reciprocal.1.pot = f32[768,256]{1,0:T(8,128)} custom-call(f32[768,256]{1,0:T(8,128)} %copy-done, f32[384,256]{1,0:T(8,128)S(1)} %get-tuple-element.10.keep, f32[384,256]{1,0:T(8,128)S(1)} %get-tuple-element.9.turn, bf16[256,256]{1,0:T(8,128)(2,1)S(1)} %copy-done.7, bf16[256,256]{1,0:T(8,128)(2,1)S(1)} %copy-done.8, bf16[384,768]{1,0:T(8,128)(2,1)S(1)} %copy-done.2, ...), custom_call_target="tpu_custom_call" | custom-call | tf_op jit(solution)/shard_map/reciprocal/pallas_call | solution.py:385
  91.9 0.0 copy-start.1
  91.9 1.1 copy-done.1
  93.1 13.9 %sample.1 = (f32[3,2048]{1,0:T(4,128)S(1)}, f32[3,2048]{1,0:T(4,128)S(1)}) custom-call(f32[32,2048]{1,0:T(8,128)S(1)} %concatenate.24.own, f32[32,2048]{1,0:T(8,128)S(1)} %collective-permute-done.before, f32[768,256]{1,0:T(8,128)S(1)} %copy-done.1), custom_call_target="tpu_custom_call" | custom-call | tf_op jit(solution)/shard_map/sample/pallas_call | solution.py:398
  107.0 0.0 copy-start.11
  107.0 0.0 copy-start.12
  107.0 5.4 %collective-permute-start.4 = (f32[3,2048]{1,0:T(4,128)S(1)}, f32[3,2048]{1,0:T(4,128)S(1)}, u32[]{:S(2)}, u32[]{:S(2)}) collective-permute-start(f32[3,2048]{1,0:T(4,128)S(1)} %get-tuple-element.8), channel_id=1, source_target_pairs={{1,0},{2,1},{3,2},{4,3},{5,4},{6,5},{7,6},{8,7},{9,8},{10,9},{11,1... | collective-permute-start | bytes 73736 | tf_op jit(solution)/shard_map/ppermute | solution.py:416
  112.4 0.0 copy-done.11
  112.5 0.0 copy-done.12
  112.5 11.1 %direct.1 = f32[3,2048]{1,0:T(4,128)S(1)} custom-call(s32[32]{0:T(128)S(1)} %copy-done.11, s32[32]{0:T(128)S(1)} %copy-done.12, s32[1]{0:T(128)S(6)} %copy.32.count, f32[32,2048]{1,0:T(8,128)S(1)} %concatenate.24.own, f32[32,2048]{1,0:T(8,128)S(1)} %collective-permute-done.before, f32[8,2048]{1,0:T(8,128)S(1)} %pad_maximum_fusion.3.after), custom_call_target="tpu_custom_call" | custom-call | tf_op jit(solution)/shard_map/direct/pallas_call | solution.py:407
  123.5 0.0 collective-permute-done.4
  123.5 0.6 add_add_fusion
  (12 shorter events, 0.2 us)
Async XLA Ops:
  2.1 3.8 %copy-start.15 = (f32[3,4,2048]{2,1,0:T(4,128)S(1)}, f32[3,4,2048]{2,1,0:T(4,128)}, u32[]{:S(2)}) copy-start(f32[3,4,2048]{2,1,0:T(4,128)} %param.25) | copy-start | bytes 294916
  2.2 45.8 %collective-permute-start.2 = (f32[384,256]{1,0:T(8,128)S(1)}, f32[384,256]{1,0:T(8,128)S(1)}, u32[]{:S(2)}, u32[]{:S(2)}) collective-permute-start(f32[384,256]{1,0:T(8,128)S(1)} %get-tuple-element.14), channel_id=1, source_target_pairs={{0,0},{1,2},{2,4},{3,6},{4,8},{5,10},{6,12},{7,14},{8,16},{9,18},{... | collective-permute-start | bytes 1179656 | tf_op jit(solution)/shard_map/ppermute | solution.py:362
  2.9 3.0 %copy-start.16 = (f32[3,4,2048]{2,1,0:T(4,128)S(1)}, f32[3,4,2048]{2,1,0:T(4,128)}, u32[]{:S(2)}) copy-start(f32[3,4,2048]{2,1,0:T(4,128)} %param.26) | copy-start | bytes 294916
  2.9 45.1 %collective-permute-start.3 = (f32[384,256]{1,0:T(8,128)S(1)}, f32[384,256]{1,0:T(8,128)S(1)}, u32[]{:S(2)}, u32[]{:S(2)}) collective-permute-start(f32[384,256]{1,0:T(8,128)S(1)} %get-tuple-element.13), channel_id=1, source_target_pairs={{0,1},{1,3},{2,5},{3,7},{4,9},{5,11},{6,13},{7,15},{8,17},{9,19},{... | collective-permute-start | bytes 1179656 | tf_op jit(solution)/shard_map/ppermute | solution.py:365
  5.9 0.7 copy-start.19
  6.0 0.7 copy-start.17
  6.0 0.7 copy-start.18
  6.0 0.8 copy-start.14
  6.6 0.8 copy-start.13
  7.8 25.4 %collective-permute-start = (f32[32,2048]{1,0:T(8,128)S(1)}, f32[32,2048]{1,0:T(8,128)S(1)}, u32[]{:S(2)}, u32[]{:S(2)}) collective-permute-start(f32[32,2048]{1,0:T(8,128)S(1)} %concatenate.24.own), channel_id=1, source_target_pairs={{0,1},{1,2},{2,3},{3,4},{4,5},{5,6},{6,7},{7,8},{8,9},{9,10},{10,1... | collective-permute-start | bytes 786440 | tf_op jit(solution)/shard_map/ppermute | solution.py:358
  9.6 8.7 %collective-permute-start.1 = (f32[6,2048]{1,0:T(8,128)S(1)}, f32[6,2048]{1,0:T(8,128)S(1)}, u32[]{:S(2)}, u32[]{:S(2)}) collective-permute-start(f32[6,2048]{1,0:T(8,128)S(1)} %pad_maximum_fusion.2), channel_id=1, source_target_pairs={{1,0},{2,1},{3,2},{4,3},{5,4},{6,5},{7,6},{8,7},{9,8},{10,9},{11,1... | collective-permute-start | bytes 147464 | tf_op jit(solution)/shard_map/ppermute | solution.py:359
  48.0 0.9 copy-start
  51.5 0.9 copy-start.7
  51.5 1.0 copy-start.8
  51.5 1.0 copy-start.9
  51.5 1.1 copy-start.10
  51.7 1.2 copy-start.2
  51.7 1.3 %copy-start.3 = (bf16[512,512]{1,0:T(8,128)(2,1)S(1)}, bf16[512,512]{1,0:T(8,128)(2,1)}, u32[]{:S(2)}) copy-start(bf16[512,512]{1,0:T(8,128)(2,1)} %constant.72.clone.fzh) | copy-start | bytes 1572868
  51.7 1.5 %copy-start.4 = (bf16[512,512]{1,0:T(8,128)(2,1)S(1)}, bf16[512,512]{1,0:T(8,128)(2,1)}, u32[]{:S(2)}) copy-start(bf16[512,512]{1,0:T(8,128)(2,1)} %constant.73.clone.fzl) | copy-start | bytes 1572868
  51.7 1.6 %copy-start.5 = (bf16[512,512]{1,0:T(8,128)(2,1)S(1)}, bf16[512,512]{1,0:T(8,128)(2,1)}, u32[]{:S(2)}) copy-start(bf16[512,512]{1,0:T(8,128)(2,1)} %constant.74.clone.bzh) | copy-start | bytes 1572868
  51.7 1.8 %copy-start.6 = (bf16[512,512]{1,0:T(8,128)(2,1)S(1)}, bf16[512,512]{1,0:T(8,128)(2,1)}, u32[]{:S(2)}) copy-start(bf16[512,512]{1,0:T(8,128)(2,1)} %constant.75.clone.bzl) | copy-start | bytes 1572868
  91.9 1.1 copy-start.1
  107.0 5.5 %copy-start.11 = (s32[32]{0:T(128)S(1)}, s32[32]{0:T(128)}, u32[]{:S(2)}) copy-start(s32[32]{0:T(128)} %home.1) | copy-start | bytes 388
  107.0 5.5 %copy-start.12 = (s32[32]{0:T(128)S(1)}, s32[32]{0:T(128)}, u32[]{:S(2)}) copy-start(s32[32]{0:T(128)} %other.1) | copy-start | bytes 388
  107.0 16.5 %collective-permute-start.4 = (f32[3,2048]{1,0:T(4,128)S(1)}, f32[3,2048]{1,0:T(4,128)S(1)}, u32[]{:S(2)}, u32[]{:S(2)}) collective-permute-start(f32[3,2048]{1,0:T(4,128)S(1)} %get-tuple-element.8), channel_id=1, source_target_pairs={{1,0},{2,1},{3,2},{4,3},{5,4},{6,5},{7,6},{8,7},{9,8},{10,9},{11,1... | collective-permute-start | bytes 73736 | tf_op jit(solution)/shard_map/ppermute | solution.py:416

commit v2 on v1

v2 whole, which is shorter than its diff:
```python
import functools

import jax
import jax.numpy as jnp
import numpy as np
from jax import lax
from jax.experimental import pallas as pl
from jax.experimental.pallas import tpu as pltpu
from jax.sharding import PartitionSpec as P

CL = 128
CLU_DEV = 16
GX = 384
GY = 256
GZ = 256
DEV = 128
ATOM_DEV = 2048
SLOTS = 32
CHUNK = 512
AXES = ("grp", "sp")

f32, bf16 = jnp.float32, jnp.bfloat16
VM = pl.BlockSpec(memory_space=pltpu.VMEM)
SM = pl.BlockSpec(memory_space=pltpu.SMEM)


def halves(table):
    high = table.astype(bf16)
    low = (table - high.astype(np.float64)).astype(bf16)
    return high, low


@functools.cache
def tables():
    t = np.arange(128)[:, None]
    d = np.where(t < 64, 2 * t, 255 - 2 * t)
    y = np.arange(GY)[None, :]
    angle = 2 * np.pi * ((d * y) % GY) / GY
    real, imag = np.cos(angle), -np.sin(angle)
    imag[0] = 1 - 2 * (np.arange(GY) % 2)
    forward_y = np.concatenate([real, imag], 0)
    scale = np.full((1, 256), 2.0)
    scale[0, 0] = scale[0, 128] = 1.0
    backward_y = forward_y.T * scale / (GX * GY * GZ)
    z = np.arange(GZ)
    angle = 2 * np.pi * ((z[:, None] * z[None, :]) % GZ) / GZ
    cos, sin = np.cos(angle), np.sin(angle)
    forward_z = np.block([[cos, -sin], [sin, cos]])
    backward_z = np.block([[cos, sin], [-sin, cos]])
    k = np.arange(GX)
    forward_x = []
    for p in range(3):
        angle = 2 * np.pi * ((k[:, None] * (3 * np.arange(128)[None, :] + p)) % GX) / GX
        forward_x += [np.cos(angle), np.sin(angle)]
    backward_x = np.concatenate(
        [np.concatenate([forward_x[2 * p].T, forward_x[2 * p + 1].T], 1) for p in range(3)], 0
    )
    forward_x = np.concatenate(forward_x, 1)
    flip_x = np.eye(GX)[:, -np.arange(GX) % GX]
    flip_z = np.eye(GZ)[:, -np.arange(GZ) % GZ]
    out = [flip_x.astype(bf16), flip_z.astype(bf16)]
    for table in (forward_y, forward_x, forward_z, backward_z, backward_x, backward_y):
        out += list(halves(table))
    return out


def split(x):
    high = x.astype(bf16)
    return high, (x - high.astype(f32)).astype(bf16)


def nn(a, b):
    return lax.dot_general(a, b, (((1,), (0,)), ((), ())), preferred_element_type=f32)


def nt(a, b):
    return lax.dot_general(a, b, (((1,), (1,)), ((), ())), preferred_element_type=f32)


def left(table_high, table_low, x):
    high, low = split(x)
    return nn(
        jnp.concatenate([table_high, table_high, table_low], 1),
        jnp.concatenate([high, low, high], 0),
    )


def right(x, table_high, table_low):
    high, low = split(x)
    return nn(
        jnp.concatenate([high, low, high], 1),
        jnp.concatenate([table_high, table_high, table_low], 0),
    )


def step_masks(base, n, kind):
    it = lax.broadcasted_iota(jnp.int32, (256, n), 0)
    at = [(base + k) & 255 for k in range(4)]
    if kind == bf16:
        it = it.astype(f32).astype(bf16)
        at = [x.astype(f32).astype(bf16) for x in at]
    return [it == x for x in at]


def pick(masks, w):
    r = jnp.where(masks[3], w[3], jnp.zeros((), w[0].dtype))
    for k in (2, 1, 0):
        r = jnp.where(masks[k], w[k], r)
    return r


def split_list(w):
    high = [x.astype(bf16) for x in w]
    return high, [(x - y.astype(f32)).astype(bf16) for x, y in zip(w, high)]


def plane_weights(local, w, step):
    step = step - local
    r = jnp.zeros_like(w[0])
    for k in range(4):
        r = jnp.where(step == k, w[k], r)
    return r


class Atoms:
    def __init__(self, shift, first, dipoles, values, slopes, plane, row, column):
        self.shift, self.first = shift, first
        self.refs = (dipoles, values, slopes, plane, row, column)

    def read(self, start):
        cols = pl.ds(pl.multiple_of(start, CHUNK), CHUNK)
        dipoles, values, slopes, plane, row, column = self.refs
        m = [dipoles[a : a + 1, cols] for a in range(3)]
        v = [[values[a, k : k + 1, cols] for k in range(4)] for a in range(3)]
        s = [[slopes[a, k : k + 1, cols] for k in range(4)] for a in range(3)]
        return row[:, cols], column[:, cols], plane[:, cols] - self.first, m, v, s


def spread_chunk(cell, start, planes, grid):
    row, column, local, m, v, s = cell.read(start)
    at_z = step_masks(column, CHUNK, bf16)
    vh, vl = [pick(at_z, w) for w in split_list(v[2])]
    sh, sl = [pick(at_z, w) for w in split_list(s[2])]
    right_side = jnp.concatenate([vh, sh, vl, vh, sl, sh], 1)
    at_y = step_masks(row, CHUNK, bf16)
    for p in planes:
        x0 = plane_weights(local, v[0], p + cell.shift)
        xs = plane_weights(local, s[0], p + cell.shift)
        a, b, c = m[0] * xs, m[1] * x0, m[2] * x0
        w1 = [a * v[1][k] + b * s[1][k] for k in range(4)]
        w2 = [c * v[1][k] for k in range(4)]
        ah, al = [pick(at_y, w) for w in split_list(w1)]
        bh, bl = [pick(at_y, w) for w in split_list(w2)]
        grid[p * 256 : p * 256 + 256, :] += nt(
            jnp.concatenate([ah, bh, ah, al, bh, bl], 1), right_side
        )


def sample_chunk(cell, start, p, stacked, out):
    row, column, local, m, v, s = cell.read(start)
    at_z = step_masks(column, CHUNK, bf16)
    vh, vl = [pick(at_z, w) for w in split_list(v[2])]
    sh, sl = [pick(at_z, w) for w in split_list(s[2])]
    at_y = step_masks(row, CHUNK, f32)
    v1, s1 = pick(at_y, v[1]), pick(at_y, s[1])
    x0 = plane_weights(local, v[0], p + cell.shift)
    xs = plane_weights(local, s[0], p + cell.shift)
    tv = nn(stacked, jnp.concatenate([vh, vl, vh], 0))
    ts = nn(stacked, jnp.concatenate([sh, sl, sh], 0))
    r = [
        xs * jnp.sum(v1 * tv, 0, keepdims=True),
        x0 * jnp.sum(s1 * tv, 0, keepdims=True),
        x0 * jnp.sum(v1 * ts, 0, keepdims=True),
    ]
    out[:, pl.ds(pl.multiple_of(start, CHUNK), CHUNK)] -= jnp.concatenate(r, 0)


def extend(parts, ext):
    for part, (positions, dipoles) in enumerate(parts):
        for c in range(CLU_DEV):
            cols = slice(c * CL, c * CL + CL)
            x = positions[:, cols]
            if part != 1:
                shift = 2.0 * (part - 1)
                x = x + jnp.where(lax.broadcasted_iota(jnp.int32, (3, CL), 0) == 0, shift, 0.0)
            ext[part * CLU_DEV + c, 0:3, :] = x
            ext[part * CLU_DEV + c, 3:6, :] = dipoles[:, cols]


def direct_slots(lo, hi, home, other, count, ext, acc):
    eye = (
        lax.broadcasted_iota(jnp.int32, (CL, CL), 0) == lax.broadcasted_iota(jnp.int32, (CL, CL), 1)
    ).astype(f32)
    which = lax.broadcasted_iota(jnp.int32, (CLU_DEV, 8, CL), 0)

    def slot(t, carry):
        h, o = home[t], other[t]
        hx = ext[h + CLU_DEV]
        ox = ext[o].T
        delta = [hx[a : a + 1, :] - ox[:, a : a + 1] for a in range(3)]
        m = [ox[:, 3 + a : 4 + a] for a in range(3)]
        q = delta[0] * delta[0] + delta[1] * delta[1] + delta[2] * delta[2]
        inverse = lax.rsqrt(q + 0.25)
        square = inverse * inverse
        self_slot = jnp.where(o == h + CLU_DEV, 1.0, 0.0)
        first = jnp.exp(-0.5 * q) * (inverse * square) * (1.0 - self_slot * eye)
        second = 3.0 * first * square
        along = second * (delta[0] * m[0] + delta[1] * m[1] + delta[2] * m[2])
        e = [jnp.sum(along * delta[a] - first * m[a], 0, keepdims=True) for a in range(3)]
        live = jnp.where(t < count[0], 0.125, 0.0)
        e = jnp.concatenate(e + [jnp.zeros((5, CL), f32)], 0) * live
        acc[...] += jnp.where(which == h, e[None], 0.0)
        return carry

    lax.fori_loop(lo, hi, slot, 0, unroll=4)


def device_id(t):
    return (t // 64, lax.rem(t, 64))


def remote(src, dst, send_sem, recv_sem, t):
    return pltpu.make_async_remote_copy(
        src_ref=src,
        dst_ref=dst,
        send_sem=send_sem,
        recv_sem=recv_sem,
        device_id=device_id(t),
        device_id_type=pl.DeviceIdType.MESH,
    )


def exchange_start(me, p, src, dst, send_sem, recv_sem):
    def send(i, c):
        t = lax.rem(me + i, DEV)
        remote(src.at[p, t], dst.at[p, me], send_sem.at[p], recv_sem.at[p], t).start()
        return c

    lax.fori_loop(1, DEV, send, 0)
    dst[p, pl.ds(me, 1)] = src[p, pl.ds(me, 1)]


def exchange_wait(p, src, sem):
    part = src.at[p, pl.ds(0, DEV - 1)]
    pltpu.make_async_copy(part, part, sem.at[p]).wait()


def to_rows(ref, p, value):
    view = ref.at[p].reshape(512, 128)
    for c in range(2):
        for h in range(2):
            view[pl.ds(2 * c + h, 128, stride=4), :] = value[
                c * 128 : c * 128 + 128, h * 128 : h * 128 + 128
            ]


def from_rows(ref, p):
    view = ref.at[p].reshape(512, 128)
    part = [view[pl.ds(k, 128, stride=4), :] for k in range(4)]
    return jnp.concatenate(part[0:2], 1), jnp.concatenate(part[2:4], 1)


def flipped(x, flip_x, flip_z):
    high, low = split(x)
    y = nn(flip_x, jnp.concatenate([high, low], 1))
    high, low = split(y[:, 0:GZ] + y[:, GZ:])
    y = nn(jnp.concatenate([high, low], 0), flip_z)
    return y[0:GX] + y[GX:]


N_TABLES = 14
N_ATOM = 7


def kernel(*refs):
    refs = list(refs)
    take = lambda n: [refs.pop(0) for _ in range(n)]
    home, other, count = take(3)
    own_refs = take(N_ATOM)
    influence, *table_hbm = take(1 + N_TABLES)
    (out,) = take(1)
    before_refs = take(N_ATOM)
    after_refs = take(2)
    table = take(N_TABLES)
    rows_in, sent, got, keep, turn = take(5)
    send1, recv1, send2, recv2, spec, other_spec, grid, ext, acc, out_before, returned = take(11)
    ss1, rs1, ss2, rs2, atom_ss, atom_rs, table_sem, rows_sem, infl_sem, back_sem = take(10)

    me = lax.axis_index("grp") * 64 + lax.axis_index("sp")
    above, below = lax.rem(me + 1, DEV), lax.rem(me + DEV - 1, DEV)
    loads = [
        pltpu.make_async_copy(a, b, table_sem.at[i])
        for i, (a, b) in enumerate(zip(table_hbm, table))
    ]
    rows_load = pltpu.make_async_copy(influence, rows_in, rows_sem)
    rows_load.start()
    for load in loads:
        load.start()
    barrier = pltpu.get_barrier_semaphore()

    def greet(i, c):
        pl.semaphore_signal(
            barrier,
            inc=1,
            device_id=device_id(lax.rem(me + i, DEV)),
            device_id_type=pl.DeviceIdType.MESH,
        )
        return c

    lax.fori_loop(1, DEV, greet, 0)
    own = Atoms(0, 3 * me, *own_refs[1:])
    before = Atoms(3, 3 * below, *before_refs[1:])
    chunks = ATOM_DEV // CHUNK

    def loop(lo, hi, f):
        def step(i, c):
            f(i * CHUNK)
            return c

        lax.fori_loop(lo, hi, step, 0)

    grid[...] = jnp.zeros_like(grid)
    out[...] = jnp.zeros_like(out)
    out_before[...] = jnp.zeros_like(out_before)
    acc[...] = jnp.zeros_like(acc)
    ext[...] = jnp.zeros_like(ext)
    loop(0, 2, lambda start: spread_chunk(own, start, range(3), grid))

    pl.semaphore_wait(barrier, DEV - 1)
    copies = [
        remote(a, b, atom_ss.at[i], atom_rs.at[i], above)
        for i, (a, b) in enumerate(zip(own_refs, before_refs))
    ]
    copies += [
        remote(a, b, atom_ss.at[N_ATOM + i], atom_rs.at[N_ATOM + i], below)
        for i, (a, b) in enumerate(zip(own_refs[:2], after_refs))
    ]
    for copy in copies:
        copy.start()
    rows_load.wait()
    lower = me < 64
    sent[...] = jnp.where(lower, rows_in[:, 1, :], rows_in[:, 0, :])
    target = jnp.where(lower, 127 - me, lax.rem(DEV - me, 64))
    infl_copy = remote(sent, got, infl_sem.at[0], infl_sem.at[1], target)
    infl_copy.start()

    loop(2, chunks, lambda start: spread_chunk(own, start, range(3), grid))
    for copy in copies:
        copy.wait()
    for load in loads:
        load.wait()
    flip_x, flip_z, fyh, fyl, fxh, fxl, fzh, fzl, bzh, bzl, bxh, bxl, byh, byl = table
    for p in range(3):
        loop(0, chunks, lambda start: spread_chunk(before, start, (p,), grid))
        to_rows(send1, p, left(fyh[...], fyl[...], grid[p * 256 : p * 256 + 256, :]))
        exchange_start(me, p, send1, recv1, ss1, rs1)

    extend(
        ((before_refs[0], before_refs[1]), (own_refs[0], own_refs[1]), (after_refs[0], after_refs[1])), ext
    )
    direct_slots(0, SLOTS // 2, home, other, count, ext, acc)
    infl_copy.wait()
    kept = jnp.where(lower, rows_in[:, 0, :], rows_in[:, 1, :])
    u, v = jnp.where(lower, kept, got[...]), jnp.where(lower, got[...], kept)
    same, turned = 0.5 * u, 0.5 * v
    both = 0.25 * (u + v)
    first = me == 0
    keep[...] = jnp.where(first, both, same) + flipped(
        jnp.where(first, both, turned), flip_x[...], flip_z[...]
    )

    @pl.when(first)
    def _():
        q = 0.25 * (rows_in[:, 0, :] - got[...])
        turn[...] = q + flipped(q, flip_x[...], flip_z[...])

    for p in range(3):
        exchange_wait(p, recv1, rs1)
        cols = slice(p * 256, p * 256 + 256)

        def stage(sign):
            real, imag = from_rows(recv1, p)
            imag = imag * sign
            x = jnp.concatenate(
                [jnp.concatenate([real, imag], 1), jnp.concatenate([imag, -real], 1)], 0
            )
            return left(fxh[:, cols], fxl[:, cols], x)

        if p == 0:
            spec[...] = stage(1.0)
        else:
            spec[...] += stage(1.0)

        @pl.when(first)
        def _():
            if p == 0:
                other_spec[...] = stage(-1.0)
            else:
                other_spec[...] += stage(-1.0)

    twice = lambda x: jnp.concatenate([x, x], 1)
    spec[...] = right(spec[...], fzh[...], fzl[...]) * twice(keep[...])

    @pl.when(first)
    def _():
        spec[...] += right(other_spec[...], fzh[...], fzl[...]) * twice(turn[...])

    back = right(spec[...], bzh[...], bzl[...])
    real, imag = back[:, 0:256], back[:, 256:512]
    x = jnp.concatenate([jnp.concatenate([real, imag], 1), jnp.concatenate([-imag, real], 1)], 0)
    high, low = split(x)
    x = jnp.concatenate([high, low, high], 0)
    for p in range(3):
        rows = slice(p * 128, p * 128 + 128)
        y = nn(jnp.concatenate([bxh[rows, :], bxh[rows, :], bxl[rows, :]], 1), x)
        to_rows(send2, p, jnp.concatenate([y[:, 0:256], y[:, 256:512]], 0))
        exchange_start(me, p, send2, recv2, ss2, rs2)

    direct_slots(SLOTS // 2, SLOTS, home, other, count, ext, acc)
    back_copy = remote(out_before, returned, back_sem.at[0], back_sem.at[1], below)
    for p in range(3):
        exchange_wait(p, recv2, rs2)
        real, imag = from_rows(recv2, p)
        high, low = split(left(byh[...], byl[...], jnp.concatenate([real, imag], 0)))
        stacked = jnp.concatenate([high, high, low], 1)
        loop(0, chunks, lambda start: sample_chunk(before, start, p, stacked, out_before))
        if p == 2:
            back_copy.start()
        loop(0, chunks, lambda start: sample_chunk(own, start, p, stacked, out))
    back_copy.wait()
    for c in range(CLU_DEV):
        cols = slice(c * CL, c * CL + CL)
        out[:, cols] += returned[:, cols] + acc[c, 0:3, :]
    for p in range(3):
        exchange_wait(p, send1, ss1)
        exchange_wait(p, send2, ss2)


def on_device(
    positions,
    dipoles,
    spline_values,
    spline_slopes,
    plane_base,
    row_base,
    column_base,
    pair_home,
    pair_other,
    pair_count,
    influence,
):
    constants = [jnp.asarray(t) for t in tables()]
    own = [
        positions,
        dipoles,
        spline_values,
        spline_slopes,
        plane_base.reshape(1, ATOM_DEV),
        row_base.reshape(1, ATOM_DEV),
        column_base.reshape(1, ATOM_DEV),
    ]
    vm = lambda x: pltpu.VMEM(x.shape, x.dtype)
    blocks = pltpu.VMEM((3, DEV, 4, 128), f32)
    return pl.pallas_call(
        kernel,
        out_shape=jax.ShapeDtypeStruct((3, ATOM_DEV), f32),
        in_specs=[SM] * 3 + [VM] * N_ATOM + [pl.BlockSpec(memory_space=pltpu.HBM)] * (1 + N_TABLES),
        out_specs=VM,
        scratch_shapes=[vm(x) for x in own]
        + [vm(x) for x in own[:2]]
        + [vm(x) for x in constants]
        + [pltpu.VMEM((GX, 2, GZ), f32)]
        + [pltpu.VMEM((GX, GZ), f32)] * 4
        + [blocks] * 4
        + [pltpu.VMEM((GX, 512), f32)] * 2
        + [
            pltpu.VMEM((768, 256), f32),
            pltpu.VMEM((48, 8, CL), f32),
            pltpu.VMEM((CLU_DEV, 8, CL), f32),
            pltpu.VMEM((3, ATOM_DEV), f32),
            pltpu.VMEM((3, ATOM_DEV), f32),
        ]
        + [pltpu.SemaphoreType.DMA((3,))] * 4
        + [pltpu.SemaphoreType.DMA((N_ATOM + 2,))] * 2
        + [pltpu.SemaphoreType.DMA((N_TABLES,)), pltpu.SemaphoreType.DMA]
        + [pltpu.SemaphoreType.DMA((2,))] * 2,
        compiler_params=pltpu.CompilerParams(
            vmem_limit_bytes=62 << 20, collective_id=0, has_side_effects=True
        ),
        name="polarization",
    )(pair_home, pair_other, pair_count, *own, influence, *constants)


def solution(mesh):
    placed = (
        P(None, AXES),
        P(None, AXES),
        P(None, None, AXES),
        P(None, None, AXES),
        P(AXES),
        P(AXES),
        P(AXES),
        P(AXES),
        P(AXES),
        P(AXES),
        P(None, AXES, None),
    )
    return jax.shard_map(
        on_device, mesh=mesh, in_specs=placed, out_specs=P(None, AXES), check_vma=False
    )
```

time: 125 us -> 89.4 us (0.72)
  starting transfers between devices: 17.6 us -> 0 us
  waiting for transfers between devices: 16.2 us -> 0 us
  Pallas kernels: 78.2 us -> 87.1 us
  local copies, waits for them, and re-layouts: 9.95 us -> 1.38 us
  other arithmetic: 1.27 us -> 0 us
    ppermute x5 -> x0, starting transfers between devices: 17.6 us -> none  [the longest x1 6.83 us: on_device(): after = lax.ppermute(near, AXES, down)]
    ppermute x5 -> x0, waiting for transfers between devices: 16.2 us -> none  [the longest x1 14.9 us: on_device(): before = lax.ppermute(own, AXES, up)]
    pallas_call x4 -> x1, Pallas kernels: 78.2 us -> 87.1 us  [on_device(): pl.pallas_call(kernel, out_shape=jax.ShapeDtypeStruct((3, ATOM_DEV), f32)...]
    slice x10 -> x0, local copies, waits for them, and re-layouts: 4.67 us -> none  [the longest x8 2.54 us: negated(): return jnp.roll(x[::-1, ::-1], (1, 1), (0, 1))]
    unnamed x40 -> x1, local copies, waits for them, and re-layouts: 4.8 us -> 1.38 us
  transfers between devices with their start and end apart: 5 -> 0, of which waited for: 2 -> 0; matrix products, arithmetic and copies ran while one was open for 0% -> 0% of each run, Pallas kernels for 21% -> 0%
where the time goes in v2:
time: 89.4 us; the launch traced here: 89.2 us
  Pallas kernels  87.1 us (97%)
  local copies, waits for them, and re-layouts  1.38 us (2%)
    pallas_call x1, Pallas kernels, on_device(): pl.pallas_call(kernel, out_shape=jax.ShapeDtypeStruct((3, ATOM_DEV), f32)...  87.1 us

profile of v2, /device:TPU:0, one launch (start us, length us, event | category | flops | bytes accessed | tf_op | source)
XLA Modules:
  0.0 89.2 jit_solution(11239823710842347072)
XLA Ops:
  0.7 87.1 %polarization.1 = f32[3,2048]{1,0:T(4,128)} custom-call(s32[32]{0:T(128)} %refs_0_.1, s32[32]{0:T(128)} %refs_1_.1, s32[1]{0:T(128)S(6)} %copy.27.refs_2_, f32[3,2048]{1,0:T(4,128)} %refs_3_.1, f32[3,2048]{1,0:T(4,128)} %refs_4_.1, f32[3,4,2048]{2,1,0:T(4,128)} %refs_5_.1, f32[3,4,2048]{2,1,0:T(4,128)} %refs_6_.1, s32[1,2048]{1,0:T(1,128)} %bitcast.3, ...), custom_call_target="tpu_custom_call" | custom-call | tf_op jit(solution)/shard_map/polarization/pallas_call | solution.py:464
  87.8 1.4 %copy.28 = f32[3,2048]{1,0:T(4,128)} copy(f32[3,2048]{1,0:T(4,128)} %polarization.1) | data formatting | bytes 49152

commit v3 on v2

--- a/solution.py
+++ b/solution.py
@@ -136,11 +136,14 @@
         return row[:, cols], column[:, cols], plane[:, cols] - self.first, m, v, s
 
 
-def spread_chunk(cell, start, planes, grid):
+def spread_chunk(cell, start, planes, grid, zt):
     row, column, local, m, v, s = cell.read(start)
     at_z = step_masks(column, CHUNK, bf16)
     vh, vl = [pick(at_z, w) for w in split_list(v[2])]
     sh, sl = [pick(at_z, w) for w in split_list(s[2])]
+    cols = pl.ds(pl.multiple_of(start, CHUNK), CHUNK)
+    for k, x in enumerate((vh, vl, sh, sl)):
+        zt[k, :, cols] = x
     right_side = jnp.concatenate([vh, sh, vl, vh, sl, sh], 1)
     at_y = step_masks(row, CHUNK, bf16)
     for p in planes:
@@ -156,23 +159,33 @@
         )
 
 
-def sample_chunk(cell, start, p, stacked, out):
+def row_tables(cell, start, yt):
     row, column, local, m, v, s = cell.read(start)
-    at_z = step_masks(column, CHUNK, bf16)
-    vh, vl = [pick(at_z, w) for w in split_list(v[2])]
-    sh, sl = [pick(at_z, w) for w in split_list(s[2])]
     at_y = step_masks(row, CHUNK, f32)
-    v1, s1 = pick(at_y, v[1]), pick(at_y, s[1])
-    x0 = plane_weights(local, v[0], p + cell.shift)
-    xs = plane_weights(local, s[0], p + cell.shift)
-    tv = nn(stacked, jnp.concatenate([vh, vl, vh], 0))
-    ts = nn(stacked, jnp.concatenate([sh, sl, sh], 0))
-    r = [
-        xs * jnp.sum(v1 * tv, 0, keepdims=True),
-        x0 * jnp.sum(s1 * tv, 0, keepdims=True),
-        x0 * jnp.sum(v1 * ts, 0, keepdims=True),
-    ]
-    out[:, pl.ds(pl.multiple_of(start, CHUNK), CHUNK)] -= jnp.concatenate(r, 0)
+    cols = pl.ds(pl.multiple_of(start, CHUNK), CHUNK)
+    yt[0, :, cols] = pick(at_y, v[1])
+    yt[1, :, cols] = pick(at_y, s[1])
+
+
+def sample_chunk(cell, start, stacked, zt, yt, out):
+    row, column, local, m, v, s = cell.read(start)
+    cols = pl.ds(pl.multiple_of(start, CHUNK), CHUNK)
+    vh, vl, sh, sl = [zt[k, :, cols] for k in range(4)]
+    v_side, s_side = jnp.concatenate([vh, vl, vh], 0), jnp.concatenate([sh, sl, sh], 0)
+    v1, s1 = yt[0, :, cols], yt[1, :, cols]
+    total = jnp.zeros((3, CHUNK), f32)
+    for p in range(3):
+        x0 = plane_weights(local, v[0], p + cell.shift)
+        xs = plane_weights(local, s[0], p + cell.shift)
+        pot = stacked[p * 256 : p * 256 + 256, :]
+        tv, ts = nn(pot, v_side), nn(pot, s_side)
+        r = [
+            xs * jnp.sum(v1 * tv, 0, keepdims=True),
+            x0 * jnp.sum(s1 * tv, 0, keepdims=True),
+            x0 * jnp.sum(v1 * ts, 0, keepdims=True),
+        ]
+        total = total + jnp.concatenate(r, 0)
+    out[:, cols] = -total
 
 
 def extend(parts, ext):
@@ -216,7 +229,7 @@
 
 
 def device_id(t):
-    return (t // 64, lax.rem(t, 64))
+    return (t >> 6, t & 63)
 
 
 def remote(src, dst, send_sem, recv_sem, t):
@@ -232,11 +245,11 @@
 
 def exchange_start(me, p, src, dst, send_sem, recv_sem):
     def send(i, c):
-        t = lax.rem(me + i, DEV)
+        t = (me + i) & (DEV - 1)
         remote(src.at[p, t], dst.at[p, me], send_sem.at[p], recv_sem.at[p], t).start()
         return c
 
-    lax.fori_loop(1, DEV, send, 0)
+    lax.fori_loop(1, DEV, send, 0, unroll=8)
     dst[p, pl.ds(me, 1)] = src[p, pl.ds(me, 1)]
 
 
@@ -284,6 +297,7 @@
     table = take(N_TABLES)
     rows_in, sent, got, keep, turn = take(5)
     send1, recv1, send2, recv2, spec, other_spec, grid, ext, acc, out_before, returned = take(11)
+    own_zt, before_zt, own_yt, before_yt, stacked = take(5)
     ss1, rs1, ss2, rs2, atom_ss, atom_rs, table_sem, rows_sem, infl_sem, back_sem = take(10)
 
     me = lax.axis_index("grp") * 64 + lax.axis_index("sp")
@@ -302,12 +316,12 @@
         pl.semaphore_signal(
             barrier,
             inc=1,
-            device_id=device_id(lax.rem(me + i, DEV)),
+            device_id=device_id((me + i) & (DEV - 1)),
             device_id_type=pl.DeviceIdType.MESH,
         )
         return c
 
-    lax.fori_loop(1, DEV, greet, 0)
+    lax.fori_loop(1, DEV, greet, 0, unroll=4)
     own = Atoms(0, 3 * me, *own_refs[1:])
     before = Atoms(3, 3 * below, *before_refs[1:])
     chunks = ATOM_DEV // CHUNK
@@ -320,11 +334,9 @@
         lax.fori_loop(lo, hi, step, 0)
 
     grid[...] = jnp.zeros_like(grid)
-    out[...] = jnp.zeros_like(out)
-    out_before[...] = jnp.zeros_like(out_before)
     acc[...] = jnp.zeros_like(acc)
     ext[...] = jnp.zeros_like(ext)
-    loop(0, 2, lambda start: spread_chunk(own, start, range(3), grid))
+    loop(0, 2, lambda start: spread_chunk(own, start, range(3), grid, own_zt))
 
     pl.semaphore_wait(barrier, DEV - 1)
     copies = [
@@ -344,14 +356,14 @@
     infl_copy = remote(sent, got, infl_sem.at[0], infl_sem.at[1], target)
     infl_copy.start()
 
-    loop(2, chunks, lambda start: spread_chunk(own, start, range(3), grid))
+    loop(2, chunks, lambda start: spread_chunk(own, start, range(3), grid, own_zt))
     for copy in copies:
         copy.wait()
     for load in loads:
         load.wait()
     flip_x, flip_z, fyh, fyl, fxh, fxl, fzh, fzl, bzh, bzl, bxh, bxl, byh, byl = table
-    for p in range(3):
-        loop(0, chunks, lambda start: spread_chunk(before, start, (p,), grid))
+    loop(0, chunks, lambda start: spread_chunk(before, start, range(3), grid, before_zt))
+    for p in range(3):
         to_rows(send1, p, left(fyh[...], fyl[...], grid[p * 256 : p * 256 + 256, :]))
         exchange_start(me, p, send1, recv1, ss1, rs1)
 
@@ -418,15 +430,16 @@
 
     direct_slots(SLOTS // 2, SLOTS, home, other, count, ext, acc)
     back_copy = remote(out_before, returned, back_sem.at[0], back_sem.at[1], below)
+    loop(0, chunks, lambda start: row_tables(before, start, before_yt))
+    loop(0, chunks, lambda start: row_tables(own, start, own_yt))
     for p in range(3):
         exchange_wait(p, recv2, rs2)
         real, imag = from_rows(recv2, p)
         high, low = split(left(byh[...], byl[...], jnp.concatenate([real, imag], 0)))
-        stacked = jnp.concatenate([high, high, low], 1)
-        loop(0, chunks, lambda start: sample_chunk(before, start, p, stacked, out_before))
-        if p == 2:
-            back_copy.start()
-        loop(0, chunks, lambda start: sample_chunk(own, start, p, stacked, out))
+        stacked[p * 256 : p * 256 + 256, :] = jnp.concatenate([high, high, low], 1)
+    loop(0, chunks, lambda start: sample_chunk(before, start, stacked, before_zt, before_yt, out_before))
+    back_copy.start()
+    loop(0, chunks, lambda start: sample_chunk(own, start, stacked, own_zt, own_yt, out))
     back_copy.wait()
     for c in range(CLU_DEV):
         cols = slice(c * CL, c * CL + CL)
@@ -480,6 +493,9 @@
             pltpu.VMEM((3, ATOM_DEV), f32),
             pltpu.VMEM((3, ATOM_DEV), f32),
         ]
+        + [pltpu.VMEM((4, 256, ATOM_DEV), bf16)] * 2
+        + [pltpu.VMEM((2, 256, ATOM_DEV), f32)] * 2
+        + [pltpu.VMEM((768, 768), bf16)]
         + [pltpu.SemaphoreType.DMA((3,))] * 4
         + [pltpu.SemaphoreType.DMA((N_ATOM + 2,))] * 2
         + [pltpu.SemaphoreType.DMA((N_TABLES,)), pltpu.SemaphoreType.DMA]

time: 89.4 us -> 69.4 us (0.78); the launches traced: 89.2 us -> 68.2 us
  Pallas kernels: 87.1 us -> 66.2 us
    pallas_call x1, Pallas kernels: 87.1 us -> 66.2 us  [on_device(): pl.pallas_call(kernel, out_shape=jax.ShapeDtypeStruct((3, ATOM_DEV), f32)...]
where the time goes in v3:
time: 69.4 us; the launch traced here: 68.2 us
  Pallas kernels  66.2 us (95%)
  local copies, waits for them, and re-layouts  1.38 us (2%)
    pallas_call x1, Pallas kernels, on_device(): pl.pallas_call(kernel, out_shape=jax.ShapeDtypeStruct((3, ATOM_DEV), f32)...  66.2 us

profile of v3, /device:TPU:0, one launch (start us, length us, event | category | flops | bytes accessed | tf_op | source)
XLA Modules:
  0.0 68.2 jit_solution(12806787389617359525)
XLA Ops:
  0.7 66.2 %polarization.1 = f32[3,2048]{1,0:T(4,128)} custom-call(s32[32]{0:T(128)} %refs_0_.1, s32[32]{0:T(128)} %refs_1_.1, s32[1]{0:T(128)S(6)} %copy.27.refs_2_, f32[3,2048]{1,0:T(4,128)} %refs_3_.1, f32[3,2048]{1,0:T(4,128)} %refs_4_.1, f32[3,4,2048]{2,1,0:T(4,128)} %refs_5_.1, f32[3,4,2048]{2,1,0:T(4,128)} %refs_6_.1, s32[1,2048]{1,0:T(1,128)} %bitcast.3, ...), custom_call_target="tpu_custom_call" | custom-call | tf_op jit(solution)/shard_map/polarization/pallas_call | solution.py:477
  66.8 1.4 %copy.28 = f32[3,2048]{1,0:T(4,128)} copy(f32[3,2048]{1,0:T(4,128)} %polarization.1) | data formatting | bytes 49152

commit v4 on v3

--- a/solution.py
+++ b/solution.py
@@ -42,10 +42,14 @@
     scale = np.full((1, 256), 2.0)
     scale[0, 0] = scale[0, 128] = 1.0
     backward_y = forward_y.T * scale / (GX * GY * GZ)
+    backward_y = np.concatenate([backward_y, backward_y[:16]], 0)
     z = np.arange(GZ)
     angle = 2 * np.pi * ((z[:, None] * z[None, :]) % GZ) / GZ
     cos, sin = np.cos(angle), np.sin(angle)
+    order = 4 * (z % 64) + z // 64
+    cos, sin = cos[order], sin[order]
     forward_z = np.block([[cos, -sin], [sin, cos]])
+    cos, sin = cos.T, sin.T
     backward_z = np.block([[cos, sin], [-sin, cos]])
     k = np.arange(GX)
     forward_x = []
@@ -93,13 +97,18 @@
     )
 
 
-def step_masks(base, n, kind):
-    it = lax.broadcasted_iota(jnp.int32, (256, n), 0)
-    at = [(base + k) & 255 for k in range(4)]
-    if kind == bf16:
-        it = it.astype(f32).astype(bf16)
-        at = [x.astype(f32).astype(bf16) for x in at]
-    return [it == x for x in at]
+FINE_Y, FINE_Z = 72, 7
+PATCH = 512
+
+
+def step_masks(base, n):
+    it = lax.broadcasted_iota(jnp.int32, (FINE_Y, n), 0)
+    return [it == base + k for k in range(4)]
+
+
+def one_hot(row, column):
+    it = lax.broadcasted_iota(jnp.int32, (256, row.shape[1]), 0)
+    return jnp.where(it == (row >> 6) * 64 + (column >> 2), 1.0, 0.0).astype(bf16)
 
 
 def pick(masks, w):
@@ -107,11 +116,6 @@
     for k in (2, 1, 0):
         r = jnp.where(masks[k], w[k], r)
     return r
-
-
-def split_list(w):
-    high = [x.astype(bf16) for x in w]
-    return high, [(x - y.astype(f32)).astype(bf16) for x, y in zip(w, high)]
 
 
 def plane_weights(local, w, step):
@@ -136,56 +140,99 @@
         return row[:, cols], column[:, cols], plane[:, cols] - self.first, m, v, s
 
 
-def spread_chunk(cell, start, planes, grid, zt):
+def fine_tables(row, column, v, s):
+    at_y = step_masks(row & 63, row.shape[1])
+    column = column & 3
+    at_z = lambda w: [plane_weights(column, w, f) for f in range(FINE_Z)]
+    return pick(at_y, v[1]), pick(at_y, s[1]), at_z(v[2]), at_z(s[2])
+
+
+def spread_chunk(cell, start, planes, patches):
     row, column, local, m, v, s = cell.read(start)
-    at_z = step_masks(column, CHUNK, bf16)
-    vh, vl = [pick(at_z, w) for w in split_list(v[2])]
-    sh, sl = [pick(at_z, w) for w in split_list(s[2])]
-    cols = pl.ds(pl.multiple_of(start, CHUNK), CHUNK)
-    for k, x in enumerate((vh, vl, sh, sl)):
-        zt[k, :, cols] = x
-    right_side = jnp.concatenate([vh, sh, vl, vh, sl, sh], 1)
-    at_y = step_masks(row, CHUNK, bf16)
+    v1, s1, v2, s2 = fine_tables(row, column, v, s)
+    hot = one_hot(row, column)
+    hot = jnp.concatenate([hot, hot], 1)
     for p in planes:
         x0 = plane_weights(local, v[0], p + cell.shift)
         xs = plane_weights(local, s[0], p + cell.shift)
-        a, b, c = m[0] * xs, m[1] * x0, m[2] * x0
-        w1 = [a * v[1][k] + b * s[1][k] for k in range(4)]
-        w2 = [c * v[1][k] for k in range(4)]
-        ah, al = [pick(at_y, w) for w in split_list(w1)]
-        bh, bl = [pick(at_y, w) for w in split_list(w2)]
-        grid[p * 256 : p * 256 + 256, :] += nt(
-            jnp.concatenate([ah, bh, ah, al, bh, bl], 1), right_side
+        a = v1 * (m[0] * xs) + s1 * (m[1] * x0)
+        b = v1 * (m[2] * x0)
+        w = [a * v2[f] + b * s2[f] for f in range(FINE_Z)] + [jnp.zeros((8, CHUNK), f32)]
+        high, low = split(jnp.concatenate(w, 0))
+        patches[p] += nt(jnp.concatenate([high, low], 1), hot)
+
+
+def roll_columns(x, step):
+    lane = lax.broadcasted_iota(jnp.int32, (x.shape[0], 128), 1) & 63
+    out = []
+    for h in range(2):
+        part = x[:, h * 128 : h * 128 + 128]
+        wrapped = lane == (0 if step == 1 else 63)
+        out.append(
+            jnp.where(
+                wrapped, pltpu.roll(part, 65 if step == 1 else 63, 1), pltpu.roll(part, step % 128, 1)
+            )
         )
-
-
-def row_tables(cell, start, yt):
+    return jnp.concatenate(out, 1)
+
+
+def swap_parts(blocks):
+    first = lax.broadcasted_iota(jnp.int32, (blocks[0].shape[0], 128), 1) < 64
+    half = [[x[:, h * 128 : h * 128 + 128] for h in range(2)] for x in blocks]
+    turned = [[pltpu.roll(x, 64, 1) for x in pair] for pair in half]
+    out = []
+    for part in range(4):
+        h, odd = part // 2, part % 2
+        row = []
+        for g in range(2):
+            even_block, odd_block = 2 * g, 2 * g + 1
+            if odd:
+                row.append(jnp.where(first, turned[even_block][h], half[odd_block][h]))
+            else:
+                row.append(jnp.where(first, half[even_block][h], turned[odd_block][h]))
+        out.append(jnp.concatenate(row, 1))
+    return out
+
+
+def patches_to_grid(patches, p, grid):
+    t = [patches[p, f * FINE_Y : f * FINE_Y + FINE_Y, :] for f in range(FINE_Z)]
+    t = [t[f] + roll_columns(t[f + 4], 1) if f < 3 else t[f] for f in range(4)]
+    grid[...] = jnp.zeros_like(grid)
+    for yb, x in enumerate(swap_parts(t)):
+        grid[64 * yb : 64 * yb + FINE_Y, :] += x
+    grid[0:8, :] += grid[256:264, :]
+    return grid[0:256, :]
+
+
+def grid_to_patches(pot, grid, stacked, p):
+    grid[...] = pot
+    t = swap_parts([grid[64 * yb : 64 * yb + FINE_Y, :] for yb in range(4)])
+    t = t + [roll_columns(t[f], -1) for f in range(3)] + [jnp.zeros((8, 256), f32)]
+    high, low = split(jnp.concatenate(t, 0))
+    stacked[p] = jnp.concatenate([high, low], 1)
+
+
+def sample_chunk(cell, start, planes, stacked, out):
     row, column, local, m, v, s = cell.read(start)
-    at_y = step_masks(row, CHUNK, f32)
-    cols = pl.ds(pl.multiple_of(start, CHUNK), CHUNK)
-    yt[0, :, cols] = pick(at_y, v[1])
-    yt[1, :, cols] = pick(at_y, s[1])
-
-
-def sample_chunk(cell, start, stacked, zt, yt, out):
-    row, column, local, m, v, s = cell.read(start)
-    cols = pl.ds(pl.multiple_of(start, CHUNK), CHUNK)
-    vh, vl, sh, sl = [zt[k, :, cols] for k in range(4)]
-    v_side, s_side = jnp.concatenate([vh, vl, vh], 0), jnp.concatenate([sh, sl, sh], 0)
-    v1, s1 = yt[0, :, cols], yt[1, :, cols]
+    v1, s1, v2, s2 = fine_tables(row, column, v, s)
+    hot = one_hot(row, column)
+    hot = jnp.concatenate([hot, hot], 0)
     total = jnp.zeros((3, CHUNK), f32)
-    for p in range(3):
+    for p in planes:
         x0 = plane_weights(local, v[0], p + cell.shift)
         xs = plane_weights(local, s[0], p + cell.shift)
-        pot = stacked[p * 256 : p * 256 + 256, :]
-        tv, ts = nn(pot, v_side), nn(pot, s_side)
+        t = nn(stacked[p], hot)
+        tv = ts = 0.0
+        for f in range(FINE_Z):
+            part = t[f * FINE_Y : f * FINE_Y + FINE_Y]
+            tv, ts = tv + part * v2[f], ts + part * s2[f]
         r = [
             xs * jnp.sum(v1 * tv, 0, keepdims=True),
             x0 * jnp.sum(s1 * tv, 0, keepdims=True),
             x0 * jnp.sum(v1 * ts, 0, keepdims=True),
         ]
         total = total + jnp.concatenate(r, 0)
-    out[:, cols] = -total
+    out[:, pl.ds(pl.multiple_of(start, CHUNK), CHUNK)] -= total
 
 
 def extend(parts, ext):
@@ -297,7 +344,7 @@
     table = take(N_TABLES)
     rows_in, sent, got, keep, turn = take(5)
     send1, recv1, send2, recv2, spec, other_spec, grid, ext, acc, out_before, returned = take(11)
-    own_zt, before_zt, own_yt, before_yt, stacked = take(5)
+    patches, stacked = take(2)
     ss1, rs1, ss2, rs2, atom_ss, atom_rs, table_sem, rows_sem, infl_sem, back_sem = take(10)
 
     me = lax.axis_index("grp") * 64 + lax.axis_index("sp")
@@ -333,10 +380,12 @@
 
         lax.fori_loop(lo, hi, step, 0)
 
-    grid[...] = jnp.zeros_like(grid)
+    patches[...] = jnp.zeros_like(patches)
+    out[...] = jnp.zeros_like(out)
+    out_before[...] = jnp.zeros_like(out_before)
     acc[...] = jnp.zeros_like(acc)
     ext[...] = jnp.zeros_like(ext)
-    loop(0, 2, lambda start: spread_chunk(own, start, range(3), grid, own_zt))
+    loop(0, 2, lambda start: spread_chunk(own, start, range(3), patches))
 
     pl.semaphore_wait(barrier, DEV - 1)
     copies = [
@@ -356,15 +405,15 @@
     infl_copy = remote(sent, got, infl_sem.at[0], infl_sem.at[1], target)
     infl_copy.start()
 
-    loop(2, chunks, lambda start: spread_chunk(own, start, range(3), grid, own_zt))
+    loop(2, chunks, lambda start: spread_chunk(own, start, range(3), patches))
     for copy in copies:
         copy.wait()
     for load in loads:
         load.wait()
     flip_x, flip_z, fyh, fyl, fxh, fxl, fzh, fzl, bzh, bzl, bxh, bxl, byh, byl = table
-    loop(0, chunks, lambda start: spread_chunk(before, start, range(3), grid, before_zt))
+    loop(0, chunks, lambda start: spread_chunk(before, start, range(3), patches))
     for p in range(3):
-        to_rows(send1, p, left(fyh[...], fyl[...], grid[p * 256 : p * 256 + 256, :]))
+        to_rows(send1, p, left(fyh[...], fyl[...], patches_to_grid(patches, p, grid)))
         exchange_start(me, p, send1, recv1, ss1, rs1)
 
     extend(
@@ -430,16 +479,14 @@
 
     direct_slots(SLOTS // 2, SLOTS, home, other, count, ext, acc)
     back_copy = remote(out_before, returned, back_sem.at[0], back_sem.at[1], below)
-    loop(0, chunks, lambda start: row_tables(before, start, before_yt))
-    loop(0, chunks, lambda start: row_tables(own, start, own_yt))
     for p in range(3):
         exchange_wait(p, recv2, rs2)
         real, imag = from_rows(recv2, p)
-        high, low = split(left(byh[...], byl[...], jnp.concatenate([real, imag], 0)))
-        stacked[p * 256 : p * 256 + 256, :] = jnp.concatenate([high, high, low], 1)
-    loop(0, chunks, lambda start: sample_chunk(before, start, stacked, before_zt, before_yt, out_before))
+        pot = left(byh[...], byl[...], jnp.concatenate([real, imag], 0))
+        grid_to_patches(pot, grid, stacked, p)
+    loop(0, chunks, lambda start: sample_chunk(before, start, range(3), stacked, out_before))
     back_copy.start()
-    loop(0, chunks, lambda start: sample_chunk(own, start, stacked, own_zt, own_yt, out))
+    loop(0, chunks, lambda start: sample_chunk(own, start, range(3), stacked, out))
     back_copy.wait()
     for c in range(CLU_DEV):
         cols = slice(c * CL, c * CL + CL)
@@ -487,15 +534,13 @@
         + [blocks] * 4
         + [pltpu.VMEM((GX, 512), f32)] * 2
         + [
-            pltpu.VMEM((768, 256), f32),
+            pltpu.VMEM((272, 256), f32),
             pltpu.VMEM((48, 8, CL), f32),
             pltpu.VMEM((CLU_DEV, 8, CL), f32),
             pltpu.VMEM((3, ATOM_DEV), f32),
             pltpu.VMEM((3, ATOM_DEV), f32),
         ]
-        + [pltpu.VMEM((4, 256, ATOM_DEV), bf16)] * 2
-        + [pltpu.VMEM((2, 256, ATOM_DEV), f32)] * 2
-        + [pltpu.VMEM((768, 768), bf16)]
+        + [pltpu.VMEM((3, PATCH, 256), f32), pltpu.VMEM((3, PATCH, 512), bf16)]
         + [pltpu.SemaphoreType.DMA((3,))] * 4
         + [pltpu.SemaphoreType.DMA((N_ATOM + 2,))] * 2
         + [pltpu.SemaphoreType.DMA((N_TABLES,)), pltpu.SemaphoreType.DMA]

time: 69.4 us -> 64.7 us (0.932)
  Pallas kernels: 66.2 us -> 61.4 us
    pallas_call x1, Pallas kernels: 66.2 us -> 61.4 us  [on_device(): pl.pallas_call(kernel, out_shape=jax.ShapeDtypeStruct((3, ATOM_DEV), f32)...]
where the time goes in v4:
time: 64.7 us; the launch traced here: 63.5 us
  Pallas kernels  61.4 us (95%)
  local copies, waits for them, and re-layouts  1.38 us (2%)
  between operations  0.66 us (1%)
    pallas_call x1, Pallas kernels, on_device(): pl.pallas_call(kernel, out_shape=jax.ShapeDtypeStruct((3, ATOM_DEV), f32)...  61.4 us
    unnamed x1, local copies, waits for them, and re-layouts  1.38 us

profile of v4, /device:TPU:0, one launch (start us, length us, event | category | flops | bytes accessed | tf_op | source)
XLA Modules:
  0.0 63.5 jit_solution(10622371195990594892)
XLA Ops:
  0.7 61.4 %polarization.1 = f32[3,2048]{1,0:T(4,128)} custom-call(s32[32]{0:T(128)} %refs_0_.1, s32[32]{0:T(128)} %refs_1_.1, s32[1]{0:T(128)S(6)} %copy.27.refs_2_, f32[3,2048]{1,0:T(4,128)} %refs_3_.1, f32[3,2048]{1,0:T(4,128)} %refs_4_.1, f32[3,4,2048]{2,1,0:T(4,128)} %refs_5_.1, f32[3,4,2048]{2,1,0:T(4,128)} %refs_6_.1, s32[1,2048]{1,0:T(1,128)} %bitcast.3, ...), custom_call_target="tpu_custom_call" | custom-call | tf_op jit(solution)/shard_map/polarization/pallas_call | solution.py:524
  62.1 1.4 %copy.28 = f32[3,2048]{1,0:T(4,128)} copy(f32[3,2048]{1,0:T(4,128)} %polarization.1) | data formatting | bytes 49152

commit v5 on v4

--- a/solution.py
+++ b/solution.py
@@ -16,7 +16,8 @@
 DEV = 128
 ATOM_DEV = 2048
 SLOTS = 32
-CHUNK = 512
+CHUNK = 1024
+SAMPLE = 1024
 AXES = ("grp", "sp")
 
 f32, bf16 = jnp.float32, jnp.bfloat16
@@ -131,8 +132,8 @@
         self.shift, self.first = shift, first
         self.refs = (dipoles, values, slopes, plane, row, column)
 
-    def read(self, start):
-        cols = pl.ds(pl.multiple_of(start, CHUNK), CHUNK)
+    def read(self, start, n):
+        cols = pl.ds(pl.multiple_of(start, n), n)
         dipoles, values, slopes, plane, row, column = self.refs
         m = [dipoles[a : a + 1, cols] for a in range(3)]
         v = [[values[a, k : k + 1, cols] for k in range(4)] for a in range(3)]
@@ -148,7 +149,7 @@
 
 
 def spread_chunk(cell, start, planes, patches):
-    row, column, local, m, v, s = cell.read(start)
+    row, column, local, m, v, s = cell.read(start, CHUNK)
     v1, s1, v2, s2 = fine_tables(row, column, v, s)
     hot = one_hot(row, column)
     hot = jnp.concatenate([hot, hot], 1)
@@ -213,11 +214,11 @@
 
 
 def sample_chunk(cell, start, planes, stacked, out):
-    row, column, local, m, v, s = cell.read(start)
+    row, column, local, m, v, s = cell.read(start, SAMPLE)
     v1, s1, v2, s2 = fine_tables(row, column, v, s)
     hot = one_hot(row, column)
     hot = jnp.concatenate([hot, hot], 0)
-    total = jnp.zeros((3, CHUNK), f32)
+    total = jnp.zeros((3, SAMPLE), f32)
     for p in planes:
         x0 = plane_weights(local, v[0], p + cell.shift)
         xs = plane_weights(local, s[0], p + cell.shift)
@@ -232,7 +233,7 @@
             x0 * jnp.sum(v1 * ts, 0, keepdims=True),
         ]
         total = total + jnp.concatenate(r, 0)
-    out[:, pl.ds(pl.multiple_of(start, CHUNK), CHUNK)] -= total
+    out[:, pl.ds(pl.multiple_of(start, SAMPLE), SAMPLE)] -= total
 
 
 def extend(parts, ext):
@@ -373,9 +374,9 @@
     before = Atoms(3, 3 * below, *before_refs[1:])
     chunks = ATOM_DEV // CHUNK
 
-    def loop(lo, hi, f):
+    def loop(lo, hi, f, n=CHUNK):
         def step(i, c):
-            f(i * CHUNK)
+            f(i * n)
             return c
 
         lax.fori_loop(lo, hi, step, 0)
@@ -385,7 +386,7 @@
     out_before[...] = jnp.zeros_like(out_before)
     acc[...] = jnp.zeros_like(acc)
     ext[...] = jnp.zeros_like(ext)
-    loop(0, 2, lambda start: spread_chunk(own, start, range(3), patches))
+    loop(0, chunks // 2, lambda start: spread_chunk(own, start, range(3), patches))
 
     pl.semaphore_wait(barrier, DEV - 1)
     copies = [
@@ -405,7 +406,7 @@
     infl_copy = remote(sent, got, infl_sem.at[0], infl_sem.at[1], target)
     infl_copy.start()
 
-    loop(2, chunks, lambda start: spread_chunk(own, start, range(3), patches))
+    loop(chunks // 2, chunks, lambda start: spread_chunk(own, start, range(3), patches))
     for copy in copies:
         copy.wait()
     for load in loads:
@@ -484,9 +485,9 @@
         real, imag = from_rows(recv2, p)
         pot = left(byh[...], byl[...], jnp.concatenate([real, imag], 0))
         grid_to_patches(pot, grid, stacked, p)
-    loop(0, chunks, lambda start: sample_chunk(before, start, range(3), stacked, out_before))
+    loop(0, ATOM_DEV // SAMPLE, lambda start: sample_chunk(before, start, range(3), stacked, out_before), SAMPLE)
     back_copy.start()
-    loop(0, chunks, lambda start: sample_chunk(own, start, range(3), stacked, out))
+    loop(0, ATOM_DEV // SAMPLE, lambda start: sample_chunk(own, start, range(3), stacked, out), SAMPLE)
     back_copy.wait()
     for c in range(CLU_DEV):
         cols = slice(c * CL, c * CL + CL)

time: 64.7 us -> 63.2 us (0.977)
  Pallas kernels: 61.4 us -> 59.9 us
    pallas_call x1, Pallas kernels: 61.4 us -> 59.9 us  [on_device(): pl.pallas_call(kernel, out_shape=jax.ShapeDtypeStruct((3, ATOM_DEV), f32)...]
where the time goes in v5:
time: 63.2 us; the launch traced here: 62 us
  Pallas kernels  59.9 us (95%)
  local copies, waits for them, and re-layouts  1.38 us (2%)
  between operations  0.66 us (1%)
    pallas_call x1, Pallas kernels, on_device(): pl.pallas_call(kernel, out_shape=jax.ShapeDtypeStruct((3, ATOM_DEV), f32)...  59.9 us
    unnamed x1, local copies, waits for them, and re-layouts  1.38 us

profile of v5, /device:TPU:0, one launch (start us, length us, event | category | flops | bytes accessed | tf_op | source)
XLA Modules:
  0.0 62.0 jit_solution(3350460636019017119)
XLA Ops:
  0.7 59.9 %polarization.1 = f32[3,2048]{1,0:T(4,128)} custom-call(s32[32]{0:T(128)} %refs_0_.1, s32[32]{0:T(128)} %refs_1_.1, s32[1]{0:T(128)S(6)} %copy.27.refs_2_, f32[3,2048]{1,0:T(4,128)} %refs_3_.1, f32[3,2048]{1,0:T(4,128)} %refs_4_.1, f32[3,4,2048]{2,1,0:T(4,128)} %refs_5_.1, f32[3,4,2048]{2,1,0:T(4,128)} %refs_6_.1, s32[1,2048]{1,0:T(1,128)} %bitcast.3, ...), custom_call_target="tpu_custom_call" | custom-call | tf_op jit(solution)/shard_map/polarization/pallas_call | solution.py:525
  60.6 1.4 %copy.28 = f32[3,2048]{1,0:T(4,128)} copy(f32[3,2048]{1,0:T(4,128)} %polarization.1) | data formatting | bytes 49152

commit v6 on v5

--- a/solution.py
+++ b/solution.py
@@ -17,7 +17,7 @@
 ATOM_DEV = 2048
 SLOTS = 32
 CHUNK = 1024
-SAMPLE = 1024
+SAMPLE = 2048
 AXES = ("grp", "sp")
 
 f32, bf16 = jnp.float32, jnp.bfloat16
@@ -297,7 +297,7 @@
         remote(src.at[p, t], dst.at[p, me], send_sem.at[p], recv_sem.at[p], t).start()
         return c
 
-    lax.fori_loop(1, DEV, send, 0, unroll=8)
+    lax.fori_loop(1, DEV, send, 0, unroll=16)
     dst[p, pl.ds(me, 1)] = src[p, pl.ds(me, 1)]
 
 
@@ -369,7 +369,7 @@
         )
         return c
 
-    lax.fori_loop(1, DEV, greet, 0, unroll=4)
+    lax.fori_loop(1, DEV, greet, 0, unroll=16)
     own = Atoms(0, 3 * me, *own_refs[1:])
     before = Atoms(3, 3 * below, *before_refs[1:])
     chunks = ATOM_DEV // CHUNK
@@ -440,32 +440,23 @@
         exchange_wait(p, recv1, rs1)
         cols = slice(p * 256, p * 256 + 256)
 
-        def stage(sign):
-            real, imag = from_rows(recv1, p)
-            imag = imag * sign
-            x = jnp.concatenate(
-                [jnp.concatenate([real, imag], 1), jnp.concatenate([imag, -real], 1)], 0
-            )
-            return left(fxh[:, cols], fxl[:, cols], x)
-
+        real, imag = from_rows(recv1, p)
+        x = jnp.concatenate([jnp.concatenate([real, imag], 1), jnp.concatenate([imag, -real], 1)], 0)
+        part = left(fxh[:, cols], fxl[:, cols], x)
         if p == 0:
-            spec[...] = stage(1.0)
+            spec[...] = part
         else:
-            spec[...] += stage(1.0)
-
-        @pl.when(first)
-        def _():
-            if p == 0:
-                other_spec[...] = stage(-1.0)
-            else:
-                other_spec[...] += stage(-1.0)
+            spec[...] += part
 
     twice = lambda x: jnp.concatenate([x, x], 1)
-    spec[...] = right(spec[...], fzh[...], fzl[...]) * twice(keep[...])
+    other_spec[...] = right(spec[...], fzh[...], fzl[...])
+    spec[...] = other_spec[...] * twice(keep[...])
 
     @pl.when(first)
     def _():
-        spec[...] += right(other_spec[...], fzh[...], fzl[...]) * twice(turn[...])
+        real = flipped(other_spec[:, 0:GZ], flip_x[...], flip_z[...])
+        imag = flipped(other_spec[:, GZ:], flip_x[...], flip_z[...])
+        spec[...] += jnp.concatenate([real, -imag], 1) * twice(turn[...])
 
     back = right(spec[...], bzh[...], bzl[...])
     real, imag = back[:, 0:256], back[:, 256:512]

time: 63.2 us -> 62.3 us (0.986)
  Pallas kernels: 59.9 us -> 59 us
    pallas_call x1, Pallas kernels: 59.9 us -> 59 us  [on_device(): pl.pallas_call(kernel, out_shape=jax.ShapeDtypeStruct((3, ATOM_DEV), f32)...]
where the time goes in v6:
time: 62.3 us; the launch traced here: 61.1 us
  Pallas kernels  59 us (95%)
  local copies, waits for them, and re-layouts  1.38 us (2%)
  between operations  0.66 us (1%)
    pallas_call x1, Pallas kernels, on_device(): pl.pallas_call(kernel, out_shape=jax.ShapeDtypeStruct((3, ATOM_DEV), f32)...  59 us
    unnamed x1, local copies, waits for them, and re-layouts  1.38 us

profile of v6, /device:TPU:0, one launch (start us, length us, event | category | flops | bytes accessed | tf_op | source)
XLA Modules:
  0.0 61.1 jit_solution(11031296795259428569)
XLA Ops:
  0.7 59.0 %polarization.1 = f32[3,2048]{1,0:T(4,128)} custom-call(s32[32]{0:T(128)} %refs_0_.1, s32[32]{0:T(128)} %refs_1_.1, s32[1]{0:T(128)S(6)} %copy.27.refs_2_, f32[3,2048]{1,0:T(4,128)} %refs_3_.1, f32[3,2048]{1,0:T(4,128)} %refs_4_.1, f32[3,4,2048]{2,1,0:T(4,128)} %refs_5_.1, f32[3,4,2048]{2,1,0:T(4,128)} %refs_6_.1, s32[1,2048]{1,0:T(1,128)} %bitcast.3, ...), custom_call_target="tpu_custom_call" | custom-call | tf_op jit(solution)/shard_map/polarization/pallas_call | solution.py:516
  59.7 1.4 %copy.28 = f32[3,2048]{1,0:T(4,128)} copy(f32[3,2048]{1,0:T(4,128)} %polarization.1) | data formatting | bytes 49152
